TPU v7x, 32 devices: a whole 2x2x4 slice. The times are simulated.
32 devices in a mesh: comm: 8 (over z, x), sub: 4 (over y, core).
Axes of the slice: x: 2, y: 2, z: 4, core: 2. Of those that a mesh axis runs over, the one named last changes fastest.
Arguments:
- features: float32 [73728, 1024], P(('comm', 'sub')), may hold values from -6 to 6
- q_weight: float32 [1024, 1024], P(('comm', 'sub')), may hold values from -0.1875 to 0.1875
- q_bias: float32 [1024], P(('comm', 'sub')), may hold values from -3 to 3
- w_weight: float32 [2048, 1024], P(('comm', 'sub')), may hold values from -0.125 to 0.125
- w_bias: float32 [1024], P(('comm', 'sub')), may hold values from -3 to 3
- nbr_index: int32 [73728, 50], P(('comm', 'sub')), may hold values from 0 to 2431
- nbr_count: int32 [73728], P(('comm', 'sub')), may hold values from 5 to 50
- importance: float32 [73728, 50], P(('comm', 'sub')), may hold values from 0.1 to 10
- send_rows: int32 [32, 32, 4], P(('comm', 'sub')), may hold values from 0 to 2303
- cotangent: float32 [73728, 1024], P(('comm', 'sub')), may hold values from -6 to 6
Outputs:
- embedding: float32 [73728, 1024], P(('comm', 'sub'))
- grad_features: float32 [73728, 1024], P(('comm', 'sub'))
- grad_q_weight: float32 [1024, 1024], P(('comm', 'sub'))
- grad_q_bias: float32 [1024], P(('comm', 'sub'))
- grad_w_weight: float32 [2048, 1024], P(('comm', 'sub'))
- grad_w_bias: float32 [1024], P(('comm', 'sub'))
All inputs are finite; a program needn't handle non-finite values.
Results may differ from a plain program's by a relative error of at most 0.0085.
Values may be sent and summed in bfloat16 or wider, within the bound.
A program may use at most 256 MiB of HBM per device.

v0:
```python
import functools
import math

import jax
import jax.numpy as jnp
from jax import lax
from jax.experimental import pallas as pl
from jax.experimental.pallas import tpu as pltpu
from jax.sharding import PartitionSpec as P

BF = jnp.bfloat16
F32 = jnp.float32
AXES = ("comm", "sub")


def build_rows(index_ref, count_ref, importance_ref, own_ref, halo_ref, first, *, rows, halo):
    his = (rows + halo + 255) // 256
    pairs = (his + 1) // 2
    fanout = index_ref.shape[0]
    at = slice(first, first + 128)
    lane = lax.broadcasted_iota(jnp.int32, (16, 128), 1)
    sublane = lax.broadcasted_iota(jnp.int32, (16, 128), 0)
    parity = (sublane >= 8).astype(jnp.int32)
    half = (lane >= 64).astype(jnp.int32)
    los = lax.broadcasted_iota(jnp.int32, (64, 256), 1).astype(BF)
    left = lax.broadcasted_iota(jnp.int32, (1, 128), 1) < 64
    hi_pattern = [(2 * t + parity).astype(BF) for t in range(pairs)]
    row_mask = [(sublane & 7) == 2 * c + half for c in range(4)]
    zero = jnp.zeros((), BF)
    one = jnp.ones((), BF)

    def slots(x):
        return jnp.concatenate([x, jnp.zeros((64 - fanout, 128), F32)], axis=0)

    def by_row(x):
        x = slots(x).T
        return jnp.concatenate([x, x], axis=1)

    index = index_ref[:, at]
    slot = lax.broadcasted_iota(jnp.int32, index.shape, 0)
    weight = jnp.where(slot < count_ref[:, at], importance_ref[:, at], 0.0)
    alpha = by_row(weight / jnp.sum(weight, axis=0, keepdims=True))
    hi = by_row((index >> 8).astype(F32))
    lo = slots((index & 255).astype(F32)).astype(BF)
    for g in range(0, 128, 16):
        tiles = []
        for s in range(2):
            left_parts, right_parts = [], []
            for c in range(4):
                r = g + s * 8 + 2 * c

                def pick(x):
                    return jnp.where(left, x[r : r + 1, :], x[r + 1 : r + 2, :]).astype(BF)

                kept = jnp.where(row_mask[c], jnp.broadcast_to(pick(alpha), (16, 128)), zero)
                hi_row = jnp.broadcast_to(pick(hi), (16, 128))
                left_parts.append(
                    jnp.concatenate(
                        [jnp.where(hi_row == hi_pattern[t], kept, zero) for t in range(pairs)], axis=0
                    )
                )
                for q in (r, r + 1):
                    right_parts.append(jnp.where(jnp.broadcast_to(lo[:, q : q + 1], (64, 256)) == los, one, zero))
            tiles.append(
                jnp.dot(
                    jnp.concatenate(left_parts, axis=1),
                    jnp.concatenate(right_parts, axis=0),
                    preferred_element_type=F32,
                )
            )
        for h in range(his):
            tile = jnp.concatenate([t[h * 8 : (h + 1) * 8, :] for t in tiles], axis=0).astype(BF)
            to = slice(first + g, first + g + 16)
            if h * 256 < rows:
                own_ref[to, h * 256 : (h + 1) * 256] = tile
            else:
                start = h * 256 - rows
                stop = min(start + 256, halo)
                halo_ref[to, start:stop] = tile[:, : stop - start]


def build_kernel(index_ref, count_ref, importance_ref, own_ref, halo_ref, *, rows, halo):
    for first in range(0, own_ref.shape[0], 128):
        build_rows(index_ref, count_ref, importance_ref, own_ref, halo_ref, first, rows=rows, halo=halo)


def build_mixing(nbr_index, nbr_count, importance, halo):
    rows, fanout = nbr_index.shape
    block = 256
    return pl.pallas_call(
        functools.partial(build_kernel, rows=rows, halo=halo),
        grid=(rows // block,),
        in_specs=[
            pl.BlockSpec((fanout, block), lambda i: (0, i)),
            pl.BlockSpec((1, block), lambda i: (0, i)),
            pl.BlockSpec((fanout, block), lambda i: (0, i)),
        ],
        out_specs=[
            pl.BlockSpec((block, rows), lambda i: (i, 0)),
            pl.BlockSpec((block, halo), lambda i: (i, 0)),
        ],
        out_shape=[
            jax.ShapeDtypeStruct((rows, rows), BF),
            jax.ShapeDtypeStruct((rows, halo), BF),
        ],
        compiler_params=pltpu.CompilerParams(vmem_limit_bytes=40 * 2**20),
        name="build_mixing",
    )(nbr_index.T, nbr_count.reshape(1, rows), importance.T)


def gelu_pair(x):
    c = math.sqrt(2.0 / math.pi)
    square = x * x
    t = jnp.tanh(x * (c + (c * 0.044715) * square))
    half = 0.5 + 0.5 * t
    slope = x * (0.5 - 0.5 * t * t) * (c + (3.0 * c * 0.044715) * square)
    return x * half, half + slope


def hidden_rows(features_ref, q, bias, sent_rows, low_ref, neigh_ref, slope_ref, sent_ref, start):
    block, width = features_ref.shape
    low_ref[...] = features_ref[...].astype(BF)
    for c in range(0, width, 256):
        pre = jnp.dot(low_ref[...], q[:, c : c + 256], preferred_element_type=F32) + bias[:, c : c + 256]
        value, slope = gelu_pair(pre)
        neigh_ref[:, c : c + 256] = value.astype(BF)
        slope_ref[:, c : c + 256] = slope.astype(BF)
    local = lax.broadcasted_iota(jnp.int32, (sent_rows.shape[0], block), 1) + start
    chosen = jnp.where(local == sent_rows, 1.0, 0.0).astype(BF)
    picked = jnp.dot(chosen, neigh_ref[...], preferred_element_type=F32)
    sent_ref[...] += picked


def gather_kernel(
    index_ref,
    count_ref,
    importance_ref,
    features_ref,
    q_ref,
    w_ref,
    bias_ref,
    send_ref,
    own_ref,
    halo_ref,
    low_ref,
    neigh_ref,
    slope_ref,
    sent_ref,
    q_full,
    w_full,
    bias_out,
    q_buf,
    w_own,
    bias_buf,
    sent_acc,
    local_sem,
    send_sem,
    recv_sem,
    *,
    subs,
    bits,
):
    i = pl.program_id(0)
    rows = own_ref.shape[1]
    halo = halo_ref.shape[1]
    builds = rows // own_ref.shape[0]
    block, width = features_ref.shape
    steps = builds + rows // block
    me = lax.axis_index("comm") * subs + lax.axis_index("sub")
    mine = [(me // (1 << b)) % 2 for b in range(bits)]
    order = list(range(bits))[::-1]

    def partner(b):
        other = me + (1 << b) * (1 - 2 * mine[b])
        return (other // subs, other % subs)

    def spot(done, part=slice(None), columns=slice(None)):
        lead = tuple(slice(None) if b in done else mine[b] for b in order)
        return lead + (part, columns)

    def copy(n, source, target, b):
        return pltpu.make_async_remote_copy(
            src_ref=source,
            dst_ref=target,
            send_sem=send_sem.at[n],
            recv_sem=recv_sem.at[n],
            device_id=partner(b),
            device_id_type=pl.DeviceIdType.MESH,
        )

    high = list(range(3, bits))[::-1]
    left, right = pl.ds(0, width // 2), pl.ds(width // 2, width // 2)
    count = [0]

    def exchange(buf, b, done, part=slice(None), columns=slice(None), source=None):
        at = buf.at[spot(done, part, columns)]
        n = count[0]
        count[0] += 1
        return copy(n, at if source is None else source, at, b)

    def chain(buf, own, split, part=slice(None)):
        groups = []
        done = []
        for b in high:
            groups.append([exchange(buf, b, done, part, source=own if not done else None)])
            done = done + [b]
        if split:
            groups.append([exchange(buf, 1, done, part, left), exchange(buf, 2, done, part, right)])
            groups.append(
                [exchange(buf, 2, done + [1], part, left), exchange(buf, 1, done + [2], part, right)]
            )
        else:
            groups.append([exchange(buf, 1, done)])
            groups.append([exchange(buf, 2, done + [1])])
        groups.append([exchange(buf, 0, done + [1, 2], part)])
        return groups

    w_rows = w_own.shape[0]
    top, bottom = pl.ds(0, w_rows // 2), pl.ds(w_rows // 2, w_rows // 2)
    chains = {
        "q": chain(q_buf, None, True),
        "bias": chain(bias_buf, None, False),
        "w0": chain(w_full, w_own.at[top], True, top),
        "w1": chain(w_full, w_own.at[bottom], True, bottom),
    }
    w_local = pltpu.make_async_copy(w_own, w_full.at[spot([])], local_sem.at[0])
    q_local = pltpu.make_async_copy(q_buf, q_full, local_sem.at[1])
    last = len(chains["q"]) - 1

    def begin(name, n):
        for c in chains[name][n]:
            c.start()

    def finish(name, n):
        for c in chains[name][n]:
            c.wait()

    def advance(name, n):
        finish(name, n)
        begin(name, n + 1)

    @pl.when(i == 0)
    def _():
        q_buf[spot([])] = q_ref[...].astype(BF)
        w_own[...] = w_ref[...].astype(BF)
        bias_buf[spot([])] = bias_ref[...]
        sent_acc[...] = jnp.zeros_like(sent_acc)
        w_local.start()
        barrier = pltpu.get_barrier_semaphore()
        for b in range(bits):
            pl.semaphore_signal(barrier, inc=1, device_id=partner(b), device_id_type=pl.DeviceIdType.MESH)
        pl.semaphore_wait(barrier, bits)
        begin("q", 0)
        begin("bias", 0)
        w_local.wait()

    events = {
        (0, 1): [("w0", -1)],
        (2, 0): [("q", 0), ("bias", 0)],
        (3, 0): [("w0", 0), ("w1", -1)],
        (3, 1): [("q", 1), ("bias", 1)],
        (4, 1): [("w0", 1)],
        (5, 0): [("q", 2), ("bias", 2)],
        (5, 1): [("w1", 0)],
        (7, 0): [("w0", 2), ("w1", 1)],
        (8, 0): [("q", 3), ("bias", 3)],
        (builds + 1, 0): [("w0", 3)],
        (builds + 2, 0): [("w1", 2)],
    }

    def happen(part):
        for (step, at), names in events.items():
            if at == part:

                @pl.when(i == step)
                def _(names=names):
                    for name, n in names:
                        if n < 0:
                            begin(name, 0)
                        else:
                            advance(name, n)

    happen(0)
    for part in range(2):
        if part == 1:
            happen(1)

        @pl.when(i < builds)
        def _(part=part):
            build_rows(
                index_ref, count_ref, importance_ref, own_ref, halo_ref, part * 128, rows=rows, halo=halo
            )

    @pl.when(i == builds)
    def _():
        finish("q", last)
        finish("bias", last)
        q_local.start()
        share = width >> bits
        for k in range(2):
            pieces = []
            for e in range(1 << bits):
                piece = bias_buf[tuple((e >> b) & 1 for b in order)]
                pieces.append(piece[0:1, k * share : (k + 1) * share])
            bias_out[k : k + 1, :] = jnp.concatenate(pieces, axis=1).astype(BF).astype(F32)
        bias_out[2:, :] = jnp.zeros((6, width), F32)

    @pl.when(i >= builds)
    def _():
        q = q_buf[...].reshape(width, width)
        hidden_rows(
            features_ref,
            q,
            bias_out[0:1, :],
            send_ref[...],
            low_ref,
            neigh_ref,
            slope_ref,
            sent_acc,
            (i - builds) * block,
        )

    @pl.when(i == steps - 1)
    def _():
        sent_ref[...] = sent_acc[...].astype(BF)
        finish("w0", last)
        advance("w1", last - 1)
        q_local.wait()
        finish("w1", last)


def gather_and_transform(features, q_weight, q_bias, w_weight, w_bias, nbr_index, nbr_count, importance, send_rows):
    comms, subs = lax.axis_size("comm"), lax.axis_size("sub")
    devices = comms * subs
    bits = devices.bit_length() - 1
    rows, width = features.shape
    fanout = nbr_index.shape[1]
    halo = send_rows.shape[1] * send_rows.shape[2]
    block = 256
    builds = rows // block
    q_rows, w_rows = q_weight.shape[0], w_weight.shape[0]
    share = q_bias.shape[0]
    bias_tile = jnp.pad(jnp.concatenate([q_bias, w_bias])[None], ((0, 7), (0, 128 - 2 * share)))
    lead = (2,) * bits

    def built(i):
        return (jnp.minimum(i, builds - 1), 0)

    def built_columns(i):
        return (0, jnp.minimum(i, builds - 1))

    def later(i):
        return (jnp.maximum(i - builds, 0), 0)

    def whole(*shape):
        return pl.BlockSpec(shape, lambda i: (0,) * len(shape))

    copies = 4 * bits + 3 * 2
    out = pl.pallas_call(
        functools.partial(gather_kernel, subs=subs, bits=bits),
        grid=(builds + rows // block,),
        in_specs=[
            pl.BlockSpec((fanout, block), built_columns),
            pl.BlockSpec((1, block), built_columns),
            pl.BlockSpec((fanout, block), built_columns),
            pl.BlockSpec((block, width), later),
            whole(q_rows, width),
            whole(w_rows, width),
            whole(8, 128),
            whole(halo, 1),
        ],
        out_specs=[
            pl.BlockSpec((block, rows), built),
            pl.BlockSpec((block, halo), built),
            pl.BlockSpec((block, width), later),
            pl.BlockSpec((block, width), later),
            pl.BlockSpec((block, width), later),
            whole(halo, width),
            pl.BlockSpec(memory_space=pl.ANY),
            pl.BlockSpec(memory_space=pl.ANY),
            whole(8, width),
        ],
        out_shape=[
            jax.ShapeDtypeStruct((rows, rows), BF),
            jax.ShapeDtypeStruct((rows, halo), BF),
            jax.ShapeDtypeStruct((rows, width), BF),
            jax.ShapeDtypeStruct((rows, width), BF),
            jax.ShapeDtypeStruct((rows, width), BF),
            jax.ShapeDtypeStruct((halo, width), BF),
            jax.ShapeDtypeStruct(lead + (q_rows, width), BF),
            jax.ShapeDtypeStruct(lead + (w_rows, width), BF),
            jax.ShapeDtypeStruct((8, width), F32),
        ],
        scratch_shapes=[
            pltpu.VMEM(lead + (q_rows, width), BF),
            pltpu.VMEM((w_rows, width), BF),
            pltpu.VMEM(lead + (8, 128), F32),
            pltpu.VMEM((halo, width), F32),
            pltpu.SemaphoreType.DMA((2,)),
            pltpu.SemaphoreType.DMA((copies,)),
            pltpu.SemaphoreType.DMA((copies,)),
        ],
        compiler_params=pltpu.CompilerParams(
            collective_id=0, has_side_effects=True, vmem_limit_bytes=48 * 2**20
        ),
        name="gather_and_transform",
    )(
        nbr_index.T,
        nbr_count.reshape(1, rows),
        importance.T,
        features,
        q_weight,
        w_weight,
        bias_tile,
        send_rows.reshape(halo, 1),
    )
    own_mix, halo_mix, low, neigh, slope, sent, q_full, w_full, biases = out
    return (
        own_mix,
        halo_mix,
        low,
        neigh,
        slope,
        sent,
        q_full.reshape(devices * q_rows, width),
        w_full.reshape(devices * w_rows, width),
        biases[0],
        biases[1],
    )


def gather_plain(features, q_weight, q_bias, w_weight, w_bias, nbr_index, nbr_count, importance, send_rows):
    rows, width = features.shape
    devices, per_peer = send_rows.shape[1:]
    halo = devices * per_peer
    own_mix, halo_mix = build_mixing(nbr_index, nbr_count, importance, halo)
    q_full = lax.all_gather(q_weight.astype(BF), AXES, axis=0, tiled=True)
    w_full = lax.all_gather(w_weight.astype(BF), AXES, axis=0, tiled=True)
    biases = doubled(jnp.stack([q_bias, w_bias]), devices)
    qbias_full = biases[:, 0].reshape(width).astype(BF).astype(F32)
    wbias_full = biases[:, 1].reshape(width).astype(BF).astype(F32)
    low = features.astype(BF)
    neigh, slope = gelu_pair(jnp.dot(low, q_full, preferred_element_type=F32) + qbias_full)
    neigh = neigh.astype(BF)
    sent = neigh[send_rows.reshape(-1)]
    return own_mix, halo_mix, low, neigh, slope.astype(BF), sent, q_full, w_full, qbias_full, wbias_full


def resident(*shape):
    return pl.BlockSpec(shape, lambda i: (0,) * len(shape), pipeline_mode=pl.Buffered(1))


def by_rows(*shape):
    return pl.BlockSpec(shape, lambda i: (i,) + (0,) * (len(shape) - 1))


def product_kernel(mix_ref, table_ref, out_ref):
    out_ref[...] = jnp.dot(mix_ref[...], table_ref[...], preferred_element_type=F32)


def pool_own(own_mix, neigh):
    rows, width = neigh.shape
    block = 384
    return pl.pallas_call(
        product_kernel,
        grid=(rows // block,),
        in_specs=[by_rows(block, rows), resident(rows, width)],
        out_specs=by_rows(block, width),
        out_shape=jax.ShapeDtypeStruct((rows, width), F32),
        compiler_params=pltpu.CompilerParams(vmem_limit_bytes=40 * 2**20),
        cost_estimate=pl.CostEstimate(
            flops=2 * rows * rows * width, bytes_accessed=2 * rows * rows + 6 * rows * width, transcendentals=0
        ),
        name="pool_own",
    )(own_mix, neigh)


def combine_kernel(
    own_ref,
    halo_ref,
    incoming_ref,
    low_ref,
    w_ref,
    bias_ref,
    cotangent_ref,
    embedding_ref,
    pooled_ref,
    grad_ref,
    grad_pooled_ref,
    sent_ref,
    bias_grad_ref,
    act_buf,
    slope_buf,
):
    i = pl.program_id(0)
    block, width = low_ref.shape
    chunk = 256

    @pl.when(i == 0)
    def _():
        sent_ref[...] = jnp.zeros_like(sent_ref)
        bias_grad_ref[...] = jnp.zeros_like(bias_grad_ref)

    pooled = own_ref[...] + jnp.dot(halo_ref[...], incoming_ref[...], preferred_element_type=F32)
    pooled_ref[...] = pooled.astype(BF)
    squares = jnp.zeros((block, 128), F32)
    dots = jnp.zeros((block, 128), F32)
    for c in range(0, width, chunk):
        at = slice(c, c + chunk)
        pre = jnp.dot(low_ref[...], w_ref[:width, at], preferred_element_type=F32)
        pre += jnp.dot(pooled_ref[...], w_ref[width:, at], preferred_element_type=F32)
        act, slope = gelu_pair(pre + bias_ref[:, at])
        act_buf[:, at] = act
        slope_buf[:, at] = slope
        square = act * act
        dot = act * cotangent_ref[:, at]
        for k in range(0, chunk, 128):
            squares += square[:, k : k + 128]
            dots += dot[:, k : k + 128]
    scale = lax.rsqrt(jnp.sum(squares, axis=1, keepdims=True) * (1.0 / width) + 1e-06)
    pull = jnp.sum(dots, axis=1, keepdims=True) * (1.0 / width) * scale * scale * scale
    for c in range(0, width, chunk):
        at = slice(c, c + chunk)
        act = act_buf[:, at]
        embedding_ref[:, at] = act * scale
        grad = slope_buf[:, at] * (cotangent_ref[:, at] * scale - act * pull)
        grad_ref[:, at] = grad.astype(BF)
        bias_grad_ref[0:1, at] += jnp.sum(grad_ref[:, at].astype(F32), axis=0, keepdims=True)
    for c in range(0, width, chunk):
        at = slice(c, c + chunk)
        back = lax.dot_general(
            grad_ref[...],
            w_ref[width + c : width + c + chunk, :],
            (((1,), (1,)), ((), ())),
            preferred_element_type=F32,
        )
        grad_pooled_ref[:, at] = back.astype(BF)
    sent_ref[...] += lax.dot_general(
        halo_ref[...], grad_pooled_ref[...], (((0,), (0,)), ((), ())), preferred_element_type=F32
    )


def combine(pooled_own, halo_mix, incoming, low, w_full, w_bias, cotangent):
    rows, width = low.shape
    halo = incoming.shape[0]
    block = 256
    return pl.pallas_call(
        combine_kernel,
        grid=(rows // block,),
        in_specs=[
            by_rows(block, width),
            by_rows(block, halo),
            resident(halo, width),
            by_rows(block, width),
            resident(2 * width, width),
            resident(1, width),
            by_rows(block, width),
        ],
        out_specs=[
            by_rows(block, width),
            by_rows(block, width),
            by_rows(block, width),
            by_rows(block, width),
            pl.BlockSpec((halo, width), lambda i: (0, 0)),
            pl.BlockSpec((8, width), lambda i: (0, 0)),
        ],
        out_shape=[
            jax.ShapeDtypeStruct((rows, width), F32),
            jax.ShapeDtypeStruct((rows, width), BF),
            jax.ShapeDtypeStruct((rows, width), BF),
            jax.ShapeDtypeStruct((rows, width), BF),
            jax.ShapeDtypeStruct((halo, width), F32),
            jax.ShapeDtypeStruct((8, width), F32),
        ],
        scratch_shapes=[pltpu.VMEM((block, width), F32), pltpu.VMEM((block, width), F32)],
        compiler_params=pltpu.CompilerParams(vmem_limit_bytes=48 * 2**20),
        cost_estimate=pl.CostEstimate(
            flops=6 * rows * width * width, bytes_accessed=22 * rows * width, transcendentals=rows * width
        ),
        name="combine",
    )(pooled_own, halo_mix, incoming, low, w_full, w_bias.reshape(1, width), cotangent)


def swap(x, bit, devices):
    return lax.ppermute(x, AXES, [(i, i ^ (1 << bit)) for i in range(devices)])


def doubled(x, devices):
    me = lax.axis_index(AXES)
    x = x[None]
    for bit in range(devices.bit_length() - 1):
        other = swap(x, bit, devices)
        first = ((me >> bit) & 1) == 0
        x = jnp.where(first, jnp.concatenate([x, other]), jnp.concatenate([other, x]))
    return x


def summed(x, devices):
    for bit in range(devices.bit_length() - 1):
        x = x + swap(x, bit, devices)
    return x


def halve(part, left, bit, devices):
    mine = (lax.axis_index(AXES) >> bit) & 1
    axis = left.index(bit)
    keep = lax.dynamic_index_in_dim(part, mine, axis, keepdims=False)
    sent = lax.dynamic_index_in_dim(part, 1 - mine, axis, keepdims=False)
    total = keep.astype(F32) + swap(sent, bit, devices).astype(F32)
    return total, [b for b in left if b != bit]


def scatter_sum(partial, devices):
    bits = list(range(devices.bit_length() - 1))[::-1]
    width = partial.shape[1]
    part = partial.reshape([2] * len(bits) + [-1, width])
    part, left = halve(part, bits, 0, devices)
    part = part.astype(BF)
    rows = part.shape[-2] // 2
    orders = ([1, 2] + list(range(3, len(bits))), [2, 1] + list(range(3, len(bits))))
    halves = [(part[..., :rows, :], left), (part[..., rows:, :], left)]
    for step in range(len(bits) - 1):
        for s in range(2):
            total, rest = halve(halves[s][0], halves[s][1], orders[s][step], devices)
            halves[s] = (total if len(rest) == 0 else total.astype(BF), rest)
    return jnp.concatenate([h[0] for h in halves], axis=0)


def shards(
    features,
    q_weight,
    q_bias,
    w_weight,
    w_bias,
    nbr_index,
    nbr_count,
    importance,
    send_rows,
    cotangent,
):
    devices = lax.axis_size(("comm", "sub"))
    rows, width = features.shape
    fanout = nbr_index.shape[1]
    per_peer = send_rows.shape[2]
    halo = devices * per_peer
    kernel_fits = devices == 32 and q_weight.shape[0] % 16 == 0
    gather = gather_and_transform if kernel_fits else gather_plain
    own_mix, halo_mix, feat_low, neigh_low, slope, outgoing, q_full, w_full, qbias_full, wbias_full = gather(
        features, q_weight, q_bias, w_weight, w_bias, nbr_index, nbr_count, importance, send_rows
    )
    targets = send_rows[0]
    incoming = lax.all_to_all(
        outgoing.reshape(devices, per_peer, width), AXES, split_axis=0, concat_axis=0, tiled=True
    )
    pooled_own = pool_own(own_mix, neigh_low)
    embedding, pooled, grad_pre_out, grad_pooled, outgoing_grad, grad_wbias = combine(
        pooled_own, halo_mix, incoming.reshape(halo, width), feat_low, w_full, wbias_full, cotangent
    )
    grad_wbias = grad_wbias[0]
    joined = jnp.concatenate([feat_low, pooled], axis=1)
    contract = (((0,), (0,)), ((), ()))
    grad_w = lax.dot_general(joined, grad_pre_out, contract, preferred_element_type=F32)
    grad_low = lax.dot_general(
        grad_pre_out, w_full[:width], (((1,), (1,)), ((), ())), preferred_element_type=F32
    )
    returned = lax.all_to_all(
        outgoing_grad.reshape(devices, per_peer, width),
        ("comm", "sub"),
        split_axis=0,
        concat_axis=0,
        tiled=True,
    )
    grad_neigh = lax.dot_general(own_mix, grad_pooled, contract, preferred_element_type=F32)
    grad_neigh = grad_neigh.at[targets.reshape(-1)].add(returned.reshape(halo, width))
    grad_pre_hidden = (slope.astype(F32) * grad_neigh).astype(BF)
    grad_q = lax.dot_general(
        feat_low, grad_pre_hidden, (((0,), (0,)), ((), ())), preferred_element_type=jnp.float32
    )
    grad_qbias = jnp.sum(grad_pre_hidden.astype(jnp.float32), axis=0)
    grad_features = grad_low + lax.dot_general(
        grad_pre_hidden, q_full, (((1,), (1,)), ((), ())), preferred_element_type=jnp.float32
    )
    me = lax.axis_index(AXES)
    bias_sums = summed(jnp.stack([grad_qbias, grad_wbias]), devices)
    bias_shards = lax.dynamic_slice_in_dim(bias_sums, me * (width // devices), width // devices, 1)
    grad_q_shard = scatter_sum(grad_q.astype(BF), devices)
    grad_w_shard = scatter_sum(grad_w.astype(BF), devices)
    grad_qbias_shard, grad_wbias_shard = bias_shards[0], bias_shards[1]
    return (
        embedding,
        grad_features,
        grad_q_shard,
        grad_qbias_shard,
        grad_w_shard,
        grad_wbias_shard,
    )


def solution(mesh):
    in_specs = (
        P(("comm", "sub"), None),
        P(("comm", "sub"), None),
        P(("comm", "sub")),
        P(("comm", "sub"), None),
        P(("comm", "sub")),
        P(("comm", "sub"), None),
        P(("comm", "sub")),
        P(("comm", "sub"), None),
        P(("comm", "sub"), None, None),
        P(("comm", "sub"), None),
    )
    out_specs = (
        P(("comm", "sub"), None),
        P(("comm", "sub"), None),
        P(("comm", "sub"), None),
        P(("comm", "sub")),
        P(("comm", "sub"), None),
        P(("comm", "sub")),
    )
    return jax.shard_map(shards, mesh=mesh, in_specs=in_specs, out_specs=out_specs, check_vma=False)
```

profile of v0, /device:TPU:0, one launch (start us, length us, event | category | flops | bytes accessed | tf_op | source)
XLA Modules:
  0.0 272.3 jit_solution(3630803529668731889)
XLA Ops:
  3.1 1.0 copy-done.1
  4.1 1.0 copy-done.2
  5.2 0.9 copy-done.3
  6.1 0.9 copy-done.4
  7.0 57.9 %gather_and_transform.1 = (bf16[2304,2304]{1,0:T(8,128)(2,1)}, bf16[2304,128]{1,0:T(8,128)(2,1)S(1)}, bf16[2304,1024]{1,0:T(8,128)(2,1)}, bf16[2304,1024]{1,0:T(...) custom-call(s32[50,2304]{1,0:T(8,128)S(1)} %bitcast.122, ...), custom_call_target="tpu_custom_call" | custom-call | tf_op jit(solution)/shard_map/gather_and_transform/pallas_call | solution.py:359
  64.9 0.8 reshape.109
  65.7 3.4 %all-to-all-start = ((bf16[32,4,1024]{2,1,0:T(4,128)(2,1)}), bf16[32,4,1024]{2,1,0:T(4,128)(2,1)S(1)}, u32[]{:S(2)}, u32[]{:S(2)}) async-start(bf16[32,4,1024]{2,1,0:T(4,128)(2,1)} %reshape.109), calls=%async_computation | async-start | bytes 524288 | tf_op jit(solution)/shard_map/all_to_all | solution.py:652
  69.1 2.3 copy-done.5
  71.4 13.5 %pool_own.1.own_ref = f32[2304,1024]{1,0:T(8,128)S(1)} custom-call(bf16[2304,2304]{1,0:T(8,128)(2,1)} %get-tuple-element.21.mix_ref, bf16[2304,1024]{1,0:T(8,128)(2,1)S(1)} %copy-done.5), custom_call_target="tpu_custom_call" | custom-call | flops 10871635968 | bytes 24772608 | tf_op jit(solution)/shard_map/pool_own/pallas_call | solution.py:464
  84.9 3.7 %copy-done.6 = f32[2304,1024]{1,0:T(8,128)} copy-done((f32[2304,1024]{1,0:T(8,128)}, f32[2304,1024]{1,0:T(8,128)S(1)}, u32[]{:S(2)}) %copy-start.6) | copy-done | bytes 9437208
  88.6 3.1 %slice.31 = bf16[1,2,2,2,2,64,1024]{6,5,4,3,2,1,0:T(8,128)(2,1)} slice(bf16[2,2,2,2,2,64,1024]{6,5,4,3,2,1,0:T(8,128)(2,1)} %get-tuple-element.26), slice={[0:1], [0:2], [0:2], [0:2], [0:2], [0:64], [0:1024]} | slice | bytes 4194304 | tf_op jit(solution)/shard_map/slice | solution.py:664
  91.8 2.2 copy-done
  94.0 29.6 %combine.1 = (f32[2304,1024]{1,0:T(8,128)}, bf16[2304,1024]{1,0:T(8,128)(2,1)}, bf16[2304,1024]{1,0:T(8,128)(2,1)}, bf16[2304,1024]{1,0:T(8,128)(2,1)}, f32[128,1024]{1,0:T(8,128)S(1)}, /*index=5*/f32[8,1024]{1,0:T(8,128)S(1)}) custom-call(f32[2304,1024]{1,0:T(8,128)} %copy-done.6, bf16[2304,128]{1,0:T(8,128)(2,1)S(1)} %get-tuple-element.23.halo_ref, ...), custom_call_target="tpu_custom_call" | custom-call | flops 14495514624 | bytes 51904512 | tf_op jit(solution)/shard_map/combine/pallas_call | solution.py:547
  123.6 16.7 %fusion.28 = f32[2304,1024]{1,0:T(8,128)} fusion(bf16[2304,2304]{1,0:T(8,128)(2,1)} %get-tuple-element.21.mix_ref, bf16[2304,1024]{1,0:T(8,128)(2,1)} %get-tuple-element.31), kind=kOutput, calls=%fused_computation.82 | convolution fusion | flops 10871635968 | bytes 24772608 | tf_op jit(solution)/shard_map/dot_general | solution.py:673
  140.3 0.9 reshape.112
  141.3 6.0 %all-to-all-start.1 = ((f32[32,4,1024]{2,1,0:T(4,128)}), f32[32,4,1024]{2,1,0:T(4,128)S(1)}, u32[]{:S(2)}, u32[]{:S(2)}) async-start(f32[32,4,1024]{2,1,0:T(4,128)} %reshape.112), calls=%async_computation.1 | async-start | bytes 1048576 | tf_op jit(solution)/shard_map/all_to_all | solution.py:666
  147.3 16.1 %fusion.5 = bf16[2048,1024]{1,0:T(8,128)(2,1)} fusion(bf16[2304,1024]{1,0:T(8,128)(2,1)} %get-tuple-element.29, bf16[2304,1024]{1,0:T(8,128)(2,1)} %get-tuple-element.35, bf16[2304,1024]{1,0:T(8,128)(2,1)} %get-tuple-element.25.low_ref), kind=kOutput, calls=%fused_computation.10 | convolution fusion | flops 9684647936 | bytes 18350080 | tf_op jit(solution)/shard_map/dot_general | solution.py:662
  163.5 9.0 %scatter_fusion = f32[2304,1024]{1,0:T(8,128)} fusion(f32[2304,1024]{1,0:T(8,128)} %fusion.28, s32[128]{0:T(128)S(1)} %fusion.22, f32[128,1024]{1,0:T(8,128)S(1)} %reshape.139), kind=kCustom, calls=%fused_computation | custom fusion | flops 131072 | bytes 1573376 | tf_op jit(solution)/shard_map/scatter-add | solution.py:674
  172.5 7.0 %convert_reduce_fusion = (f32[1024]{0:T(1024)S(1)}, bf16[2304,1024]{1,0:T(8,128)(2,1)S(1)}) fusion(f32[2304,1024]{1,0:T(8,128)} %scatter_fusion, bf16[2304,1024]{1,0:T(8,128)(2,1)} %get-tuple-element.30), kind=kLoop, calls=%fused_computation.5 | loop fusion | flops 11795456 | bytes 18878464 | tf_op jit(solution)/shard_map/reduce_sum | solution.py:679
  179.7 2.9 %constant_dynamic-slice_fusion.2 = (bf16[2,2,2,2,1,64,1024]{6,5,4,3,2,1,0:T(8,128)(2,1)S(1)}, bf16[2,2,2,2,1,64,1024]{6,5,4,3,2,1,0:T(8,128)(2,1)S(1)}) fusion(bf16[2,2,2,2,2,64,1024]{6,5,4,3,2,1,0:T(8,128)(2,1)} %bitcast.125, s32[]{:T(128)S(6)} %select_n.82, s32[]{:T(128)S(6)} %select_n.83), kind=kLoop, calls=%fused_computation.66 | loop fusion | bytes 8388616 | tf_op jit(solution)/shard_map/jit(dynamic_index_in_dim)/dynamic_slice | solution.py:607
  183.4 1.7 collective-permute-start.10
  185.1 10.0 %fusion.27 = f32[2304,1024]{1,0:T(8,128)} fusion(bf16[2304,1024]{1,0:T(8,128)(2,1)} %get-tuple-element.29, bf16[1024,1024]{1,0:T(8,128)(2,1)S(1)} %bitcast.127), kind=kOutput, calls=%fused_computation.81 | convolution fusion | flops 4831838208 | bytes 16252928 | tf_op jit(solution)/shard_map/dot_general | solution.py:663
  195.1 1.5 collective-permute-start.11
  196.6 5.4 %convolution_convert_fusion = bf16[1024,1024]{1,0:T(8,128)(2,1)S(1)} fusion(bf16[2304,1024]{1,0:T(8,128)(2,1)S(1)} %bitcast.134, bf16[2304,1024]{1,0:T(8,128)(2,1)S(1)} %get-tuple-element.37), kind=kOutput, calls=%fused_computation.15 | convolution fusion | flops 4832886784 | bytes 11534336 | tf_op jit(solution)/shard_map/dot_general | solution.py:676
  202.0 1.5 collective-permute-start.12
  204.0 1.8 collective-permute-done.12
  205.8 2.4 collective-permute-start.13
  208.2 10.0 %convolution_add_fusion = f32[2304,1024]{1,0:T(8,128)} fusion(f32[2304,1024]{1,0:T(8,128)} %fusion.27, bf16[2304,1024]{1,0:T(8,128)(2,1)S(1)} %get-tuple-element.37, bf16[1024,1024]{1,0:T(8,128)(2,1)S(1)} %bitcast.124), kind=kOutput, calls=%fused_computation.7 | convolution fusion | flops 4834197504 | bytes 25690112 | tf_op jit(solution)/shard_map/dot_general | solution.py:680
  220.6 1.1 fusion.4
  221.9 1.5 collective-permute-start.15
  223.5 1.6 collective-permute-start.19
  225.0 3.6 %collective-permute-done.1 = bf16[2,2,2,16,1024]{4,3,0,1,2:T(8,128)(2,1)S(1)} collective-permute-done((bf16[2,2,2,16,1024]{4,3,0,1,2:T(8,128)(2,1)S(1)}, bf16[2,2,2,16,1024]{4,3,0,1,2:T(8,128)(2,1)S(1)}, u32[]{:S(2)}, u32[]{:S(2)}) %collective-permute-start.1) | collective-permute-done | bytes 262176 | tf_op jit(solution)/shard_map/ppermute | solution.py:585
  229.4 1.5 collective-permute-start.6
  230.9 9.7 %collective-permute-done.2 = bf16[2,2,16,1024]{3,2,0,1:T(8,128)(2,1)S(1)} collective-permute-done((bf16[2,2,16,1024]{3,2,0,1:T(8,128)(2,1)S(1)}, bf16[2,2,16,1024]{3,2,0,1:T(8,128)(2,1)S(1)}, u32[]{:S(2)}, u32[]{:S(2)}) %collective-permute-start.2) | collective-permute-done | bytes 131104 | tf_op jit(solution)/shard_map/ppermute | solution.py:585
  240.6 1.5 collective-permute-start.3
  242.9 2.1 collective-permute-done.3
  245.6 1.3 collective-permute-done.7
  246.9 1.2 collective-permute-start.8
  248.1 1.8 collective-permute-done.4
  249.9 2.2 collective-permute-done.8
  253.7 1.7 collective-permute-start.20
  255.4 4.1 %collective-permute-done.16 = bf16[2,2,32,1024]{3,2,0,1:T(8,128)(2,1)S(1)} collective-permute-done((bf16[2,2,32,1024]{3,2,0,1:T(8,128)(2,1)S(1)}, bf16[2,2,32,1024]{3,2,0,1:T(8,128)(2,1)S(1)}, u32[]{:S(2)}, u32[]{:S(2)}) %collective-permute-start.16) | collective-permute-done | bytes 262176 | tf_op jit(solution)/shard_map/ppermute | solution.py:585
  260.2 1.6 collective-permute-start.21
  261.9 3.0 %collective-permute-done.17 = bf16[2,32,1024]{2,1,0:T(8,128)(2,1)S(1)} collective-permute-done((bf16[2,32,1024]{2,1,0:T(8,128)(2,1)S(1)}, bf16[2,32,1024]{2,1,0:T(8,128)(2,1)S(1)}, u32[]{:S(2)}, u32[]{:S(2)}) %collective-permute-start.17) | collective-permute-done | bytes 131104 | tf_op jit(solution)/shard_map/ppermute | solution.py:585
  264.9 0.8 collective-permute-start.18
  266.3 1.7 collective-permute-start.22
  268.0 2.4 collective-permute-done.18
  270.4 1.1 collective-permute-done.22
  (96 shorter events, 12.5 us)
Async XLA Ops:
  3.1 1.0 copy-start.1
  4.1 1.0 copy-start.2
  5.2 0.9 copy-start.3
  6.1 0.9 copy-start.4
  65.7 26.0 %all-to-all-start = ((bf16[32,4,1024]{2,1,0:T(4,128)(2,1)}), bf16[32,4,1024]{2,1,0:T(4,128)(2,1)S(1)}, u32[]{:S(2)}, u32[]{:S(2)}) async-start(bf16[32,4,1024]{2,1,0:T(4,128)(2,1)} %reshape.109), calls=%async_computation | async-start | bytes 524288 | tf_op jit(solution)/shard_map/all_to_all | solution.py:652
  69.1 2.3 copy-start.5
  84.9 3.7 %copy-start.6 = (f32[2304,1024]{1,0:T(8,128)}, f32[2304,1024]{1,0:T(8,128)S(1)}, u32[]{:S(2)}) copy-start(f32[2304,1024]{1,0:T(8,128)S(1)} %pool_own.1.own_ref) | copy-start | bytes 28311556
  91.8 2.2 copy-start
  141.3 22.1 %all-to-all-start.1 = ((f32[32,4,1024]{2,1,0:T(4,128)}), f32[32,4,1024]{2,1,0:T(4,128)S(1)}, u32[]{:S(2)}, u32[]{:S(2)}) async-start(f32[32,4,1024]{2,1,0:T(4,128)} %reshape.112), calls=%async_computation.1 | async-start | bytes 1048576 | tf_op jit(solution)/shard_map/all_to_all | solution.py:666
  179.6 3.8 %collective-permute-start.9 = (f32[2,1024]{1,0:T(2,128)S(1)}, f32[2,1024]{1,0:T(2,128)S(1)}, u32[]{:S(2)}, u32[]{:S(2)}) collective-permute-start(f32[2,1024]{1,0:T(2,128)S(1)} %pad_maximum_fusion.2), channel_id=1, source_target_pairs={{0,1},{1,0},{2,3},{3,2},{4,5},{5,4},{6,7},{7,6},{8,9},{9,8},{10,11... | collective-permute-start | bytes 24584 | tf_op jit(solution)/shard_map/ppermute | solution.py:585
  179.7 5.4 %copy-start.7 = (bf16[1,2,2,2,2,64,1024]{6,5,4,3,2,1,0:T(8,128)(2,1)S(1)}, bf16[1,2,2,2,2,64,1024]{6,5,4,3,2,1,0:T(8,128)(2,1)}, u32[]{:S(2)}) copy-start(bf16[1,2,2,2,2,64,1024]{6,5,4,3,2,1,0:T(8,128)(2,1)} %slice.31) | copy-start | bytes 6291460
  182.7 14.0 %slice-start = ((s8[4718592]{0:T(1024)(128)(4,1)}), s8[4194304]{0:T(1024)(128)(4,1)S(1)}, s32[]{:S(2)}) async-start(s8[4718592]{0:T(1024)(128)(4,1)} %bitcast.133), calls=%async_computation.2 | async-start | bytes 8388608
  182.9 37.7 %collective-permute-start.14 = (bf16[2,2,2,2,64,1024]{5,4,0,1,3,2:T(8,128)(2,1)S(1)}, bf16[2,2,2,2,64,1024]{5,4,0,1,3,2:T(8,128)(2,1)S(1)}, u32[]{:S(2)}, u32[]{:S(2)}) collective-permute-start(bf16[2,2,2,2,64,1024]{5,4,0,1,3,2:T(8,128)(2,1)S(1)} %bitcast.128), channel_id=1, source_target_pairs={{0,1},{1,0},{2,3},{3,2},{4,5},{5,4},{6,7},{7,6},{8,9},{9,8},{10,11... | collective-permute-start | bytes 6291464 | tf_op jit(solution)/shard_map/ppermute | solution.py:585
  183.4 11.7 %collective-permute-start.10 = (f32[2,1024]{1,0:T(2,128)S(1)}, f32[2,1024]{1,0:T(2,128)S(1)}, u32[]{:S(2)}, u32[]{:S(2)}) collective-permute-start(f32[2,1024]{1,0:T(2,128)S(1)} %fusion.24), channel_id=1, source_target_pairs={{0,2},{1,3},{2,0},{3,1},{4,6},{5,7},{6,4},{7,5},{8,10},{9,11},{10,... | collective-permute-start | bytes 24584 | tf_op jit(solution)/shard_map/ppermute | solution.py:585
  185.1 11.6 %slice-start.1 = ((s8[4718592]{0:T(1024)(128)(4,1)}), s8[524288]{0:T(1024)(128)(4,1)S(1)}, s32[]{:S(2)}) async-start(s8[4718592]{0:T(1024)(128)(4,1)} %bitcast.133), calls=%async_computation.3 | async-start | bytes 1048576
  195.1 6.9 %collective-permute-start.11 = (f32[2,1024]{1,0:T(2,128)S(1)}, f32[2,1024]{1,0:T(2,128)S(1)}, u32[]{:S(2)}, u32[]{:S(2)}) collective-permute-start(f32[2,1024]{1,0:T(2,128)S(1)} %fusion.38), channel_id=1, source_target_pairs={{0,4},{1,5},{2,6},{3,7},{4,0},{5,1},{6,2},{7,3},{8,12},{9,13},{10,... | collective-permute-start | bytes 24584 | tf_op jit(solution)/shard_map/ppermute | solution.py:585
  202.0 3.7 %collective-permute-start.12 = (f32[2,1024]{1,0:T(2,128)S(1)}, f32[2,1024]{1,0:T(2,128)S(1)}, u32[]{:S(2)}, u32[]{:S(2)}) collective-permute-start(f32[2,1024]{1,0:T(2,128)S(1)} %add.211), channel_id=1, source_target_pairs={{0,8},{1,9},{2,10},{3,11},{4,12},{5,13},{6,14},{7,15},{8,0},{9,1},... | collective-permute-start | bytes 24584 | tf_op jit(solution)/shard_map/ppermute | solution.py:585
  203.9 14.9 %collective-permute-start = (bf16[2,2,2,2,32,1024]{5,4,0,1,3,2:T(8,128)(2,1)S(1)}, bf16[2,2,2,2,32,1024]{5,4,0,1,3,2:T(8,128)(2,1)S(1)}, u32[]{:S(2)}, u32[]{:S(2)}) collective-permute-start(bf16[2,2,2,2,32,1024]{5,4,0,1,3,2:T(8,128)(2,1)S(1)} %bitcast.129), channel_id=1, source_target_pairs={{0,1},{1,0},{2,3},{3,2},{4,5},{5,4},{6,7},{7,6},{8,9},{9,8},{10,11... | collective-permute-start | bytes 3145736 | tf_op jit(solution)/shard_map/ppermute | solution.py:585
  205.8 12.4 %collective-permute-start.13 = (f32[2,1024]{1,0:T(2,128)S(1)}, f32[2,1024]{1,0:T(2,128)S(1)}, u32[]{:S(2)}, u32[]{:S(2)}) collective-permute-start(f32[2,1024]{1,0:T(2,128)S(1)} %add.212), channel_id=1, source_target_pairs={{0,16},{1,17},{2,18},{3,19},{4,20},{5,21},{6,22},{7,23},{8,24},{9,... | collective-permute-start | bytes 24584 | tf_op jit(solution)/shard_map/ppermute | solution.py:585
  219.3 9.3 %collective-permute-start.1 = (bf16[2,2,2,16,1024]{4,3,0,1,2:T(8,128)(2,1)S(1)}, bf16[2,2,2,16,1024]{4,3,0,1,2:T(8,128)(2,1)S(1)}, u32[]{:S(2)}, u32[]{:S(2)}) collective-permute-start(bf16[2,2,2,16,1024]{4,3,0,1,2:T(8,128)(2,1)S(1)} %dynamic-slice_bitcast_fusion.5), channel_id=1, source_target_pairs={{0,2},{1,3},{2,0},{3,1},{4,6},{5,7},{6,4},{7,5},{8,10},{9,11},{10,... | collective-permute-start | bytes 786440 | tf_op jit(solution)/shard_map/ppermute | solution.py:585
  219.9 9.4 %collective-permute-start.5 = (bf16[2,2,2,16,1024]{4,3,0,1,2:T(8,128)(2,1)S(1)}, bf16[2,2,2,16,1024]{4,3,0,1,2:T(8,128)(2,1)S(1)}, u32[]{:S(2)}, u32[]{:S(2)}) collective-permute-start(bf16[2,2,2,16,1024]{4,3,0,1,2:T(8,128)(2,1)S(1)} %dynamic-slice_bitcast_fusion.4), channel_id=1, source_target_pairs={{0,4},{1,5},{2,6},{3,7},{4,0},{5,1},{6,2},{7,3},{8,12},{9,13},{10,... | collective-permute-start | bytes 786440 | tf_op jit(solution)/shard_map/ppermute | solution.py:585
  221.9 30.9 %collective-permute-start.15 = (bf16[2,2,2,32,1024]{4,3,0,1,2:T(8,128)(2,1)S(1)}, bf16[2,2,2,32,1024]{4,3,0,1,2:T(8,128)(2,1)S(1)}, u32[]{:S(2)}, u32[]{:S(2)}) collective-permute-start(bf16[2,2,2,32,1024]{4,3,0,1,2:T(8,128)(2,1)S(1)} %dynamic-slice_bitcast_fusion.1), channel_id=1, source_target_pairs={{0,2},{1,3},{2,0},{3,1},{4,6},{5,7},{6,4},{7,5},{8,10},{9,11},{10,... | collective-permute-start | bytes 1572872 | tf_op jit(solution)/shard_map/ppermute | solution.py:585
  223.5 30.0 %collective-permute-start.19 = (bf16[2,2,2,32,1024]{4,3,0,1,2:T(8,128)(2,1)S(1)}, bf16[2,2,2,32,1024]{4,3,0,1,2:T(8,128)(2,1)S(1)}, u32[]{:S(2)}, u32[]{:S(2)}) collective-permute-start(bf16[2,2,2,32,1024]{4,3,0,1,2:T(8,128)(2,1)S(1)} %dynamic-slice_bitcast_fusion), channel_id=1, source_target_pairs={{0,4},{1,5},{2,6},{3,7},{4,0},{5,1},{6,2},{7,3},{8,12},{9,13},{10,... | collective-permute-start | bytes 1572872 | tf_op jit(solution)/shard_map/ppermute | solution.py:585
  228.7 11.8 %collective-permute-start.2 = (bf16[2,2,16,1024]{3,2,0,1:T(8,128)(2,1)S(1)}, bf16[2,2,16,1024]{3,2,0,1:T(8,128)(2,1)S(1)}, u32[]{:S(2)}, u32[]{:S(2)}) collective-permute-start(bf16[2,2,16,1024]{3,2,0,1:T(8,128)(2,1)S(1)} %dynamic-slice_bitcast_fusion.9), channel_id=1, source_target_pairs={{0,4},{1,5},{2,6},{3,7},{4,0},{5,1},{6,2},{7,3},{8,12},{9,13},{10,... | collective-permute-start | bytes 393224 | tf_op jit(solution)/shard_map/ppermute | solution.py:585
  229.4 12.7 %collective-permute-start.6 = (bf16[2,2,16,1024]{3,2,0,1:T(8,128)(2,1)S(1)}, bf16[2,2,16,1024]{3,2,0,1:T(8,128)(2,1)S(1)}, u32[]{:S(2)}, u32[]{:S(2)}) collective-permute-start(bf16[2,2,16,1024]{3,2,0,1:T(8,128)(2,1)S(1)} %dynamic-slice_bitcast_fusion.8), channel_id=1, source_target_pairs={{0,2},{1,3},{2,0},{3,1},{4,6},{5,7},{6,4},{7,5},{8,10},{9,11},{10,... | collective-permute-start | bytes 393224 | tf_op jit(solution)/shard_map/ppermute | solution.py:585
  240.6 4.3 %collective-permute-start.3 = (bf16[2,16,1024]{2,1,0:T(8,128)(2,1)S(1)}, bf16[2,16,1024]{2,1,0:T(8,128)(2,1)S(1)}, u32[]{:S(2)}, u32[]{:S(2)}) collective-permute-start(bf16[2,16,1024]{2,1,0:T(8,128)(2,1)S(1)} %dynamic-slice_bitcast_fusion.13), channel_id=1, source_target_pairs={{0,8},{1,9},{2,10},{3,11},{4,12},{5,13},{6,14},{7,15},{8,0},{9,1},... | collective-permute-start | bytes 196616 | tf_op jit(solution)/shard_map/ppermute | solution.py:585
  242.2 4.7 %collective-permute-start.7 = (bf16[2,16,1024]{2,1,0:T(8,128)(2,1)S(1)}, bf16[2,16,1024]{2,1,0:T(8,128)(2,1)S(1)}, u32[]{:S(2)}, u32[]{:S(2)}) collective-permute-start(bf16[2,16,1024]{2,1,0:T(8,128)(2,1)S(1)} %dynamic-slice_bitcast_fusion.12), channel_id=1, source_target_pairs={{0,8},{1,9},{2,10},{3,11},{4,12},{5,13},{6,14},{7,15},{8,0},{9,1},... | collective-permute-start | bytes 196616 | tf_op jit(solution)/shard_map/ppermute | solution.py:585
  245.0 4.9 %collective-permute-start.4 = (bf16[16,1024]{1,0:T(8,128)(2,1)S(1)}, bf16[16,1024]{1,0:T(8,128)(2,1)S(1)}, u32[]{:S(2)}, u32[]{:S(2)}) collective-permute-start(bf16[16,1024]{1,0:T(8,128)(2,1)S(1)} %dynamic-slice_bitcast_fusion.15), channel_id=1, source_target_pairs={{0,16},{1,17},{2,18},{3,19},{4,20},{5,21},{6,22},{7,23},{8,24},{9,... | collective-permute-start | bytes 98312 | tf_op jit(solution)/shard_map/ppermute | solution.py:585
  246.9 5.2 %collective-permute-start.8 = (bf16[16,1024]{1,0:T(8,128)(2,1)S(1)}, bf16[16,1024]{1,0:T(8,128)(2,1)S(1)}, u32[]{:S(2)}, u32[]{:S(2)}) collective-permute-start(bf16[16,1024]{1,0:T(8,128)(2,1)S(1)} %dynamic-slice_bitcast_fusion.14), channel_id=1, source_target_pairs={{0,16},{1,17},{2,18},{3,19},{4,20},{5,21},{6,22},{7,23},{8,24},{9,... | collective-permute-start | bytes 98312 | tf_op jit(solution)/shard_map/ppermute | solution.py:585
  253.1 6.4 %collective-permute-start.16 = (bf16[2,2,32,1024]{3,2,0,1:T(8,128)(2,1)S(1)}, bf16[2,2,32,1024]{3,2,0,1:T(8,128)(2,1)S(1)}, u32[]{:S(2)}, u32[]{:S(2)}) collective-permute-start(bf16[2,2,32,1024]{3,2,0,1:T(8,128)(2,1)S(1)} %dynamic-slice_bitcast_fusion.3), channel_id=1, source_target_pairs={{0,4},{1,5},{2,6},{3,7},{4,0},{5,1},{6,2},{7,3},{8,12},{9,13},{10,... | collective-permute-start | bytes 786440 | tf_op jit(solution)/shard_map/ppermute | solution.py:585
  253.7 6.4 %collective-permute-start.20 = (bf16[2,2,32,1024]{3,2,0,1:T(8,128)(2,1)S(1)}, bf16[2,2,32,1024]{3,2,0,1:T(8,128)(2,1)S(1)}, u32[]{:S(2)}, u32[]{:S(2)}) collective-permute-start(bf16[2,2,32,1024]{3,2,0,1:T(8,128)(2,1)S(1)} %dynamic-slice_bitcast_fusion.2), channel_id=1, source_target_pairs={{0,2},{1,3},{2,0},{3,1},{4,6},{5,7},{6,4},{7,5},{8,10},{9,11},{10,... | collective-permute-start | bytes 786440 | tf_op jit(solution)/shard_map/ppermute | solution.py:585
  259.6 5.2 %collective-permute-start.17 = (bf16[2,32,1024]{2,1,0:T(8,128)(2,1)S(1)}, bf16[2,32,1024]{2,1,0:T(8,128)(2,1)S(1)}, u32[]{:S(2)}, u32[]{:S(2)}) collective-permute-start(bf16[2,32,1024]{2,1,0:T(8,128)(2,1)S(1)} %dynamic-slice_bitcast_fusion.7), channel_id=1, source_target_pairs={{0,8},{1,9},{2,10},{3,11},{4,12},{5,13},{6,14},{7,15},{8,0},{9,1},... | collective-permute-start | bytes 393224 | tf_op jit(solution)/shard_map/ppermute | solution.py:585
  260.2 6.0 %collective-permute-start.21 = (bf16[2,32,1024]{2,1,0:T(8,128)(2,1)S(1)}, bf16[2,32,1024]{2,1,0:T(8,128)(2,1)S(1)}, u32[]{:S(2)}, u32[]{:S(2)}) collective-permute-start(bf16[2,32,1024]{2,1,0:T(8,128)(2,1)S(1)} %dynamic-slice_bitcast_fusion.6), channel_id=1, source_target_pairs={{0,8},{1,9},{2,10},{3,11},{4,12},{5,13},{6,14},{7,15},{8,0},{9,1},... | collective-permute-start | bytes 393224 | tf_op jit(solution)/shard_map/ppermute | solution.py:585
  264.9 5.5 %collective-permute-start.18 = (bf16[32,1024]{1,0:T(8,128)(2,1)S(1)}, bf16[32,1024]{1,0:T(8,128)(2,1)S(1)}, u32[]{:S(2)}, u32[]{:S(2)}) collective-permute-start(bf16[32,1024]{1,0:T(8,128)(2,1)S(1)} %dynamic-slice_bitcast_fusion.11), channel_id=1, source_target_pairs={{0,16},{1,17},{2,18},{3,19},{4,20},{5,21},{6,22},{7,23},{8,24},{9,... | collective-permute-start | bytes 196616 | tf_op jit(solution)/shard_map/ppermute | solution.py:585
  266.3 5.2 %collective-permute-start.22 = (bf16[32,1024]{1,0:T(8,128)(2,1)S(1)}, bf16[32,1024]{1,0:T(8,128)(2,1)S(1)}, u32[]{:S(2)}, u32[]{:S(2)}) collective-permute-start(bf16[32,1024]{1,0:T(8,128)(2,1)S(1)} %dynamic-slice_bitcast_fusion.10), channel_id=1, source_target_pairs={{0,16},{1,17},{2,18},{3,19},{4,20},{5,21},{6,22},{7,23},{8,24},{9,... | collective-permute-start | bytes 196616 | tf_op jit(solution)/shard_map/ppermute | solution.py:585
where the time goes:
time: 273 us; the launch traced here: 272 us
  Pallas kernels  101 us (37%)
  matrix products  58.2 us (21%)
  starting transfers between devices  34.1 us (12%)
  waiting for transfers between devices  33.7 us (12%)
  local copies, waits for them, and re-layouts  23.6 us (9%)
  other arithmetic  20.7 us (8%)
    pallas_call x1, Pallas kernels, gather_and_transform(): pl.pallas_call(functools.partial(gather_kernel, subs=subs, bits=bits), gr...  57.9 us
    ppermute x23, waiting for transfers between devices, swap(): return lax.ppermute(x, AXES, [(i, i ^ 1 << bit) for i in range(devices)])  33.7 us
    pallas_call x1, Pallas kernels, combine(): pl.pallas_call(combine_kernel, grid=(rows // block,), in_specs=[by_rows(b...  29.6 us
    ppermute x23, starting transfers between devices, swap(): return lax.ppermute(x, AXES, [(i, i ^ 1 << bit) for i in range(devices)])  24.8 us
    dot_general x1, matrix products, shards(): lax.dot_general(own_mix, grad_pooled, contract, preferred_element_type=F32)  16.7 us
    dot_general x1, matrix products, shards(): lax.dot_general(joined, grad_pre_out, contract, preferred_element_type=F32)  16.1 us
    pallas_call x1, Pallas kernels, pool_own(): pl.pallas_call(product_kernel, grid=(rows // block,), in_specs=[by_rows(b...  13.5 us
    unnamed x21, local copies, waits for them, and re-layouts  13 us
  transfers between devices with their start and end apart: 25, of which 13 were waited for; matrix products, arithmetic and copies ran while one was open for 19% of the time, Pallas kernels for 5%

commit v1 on v0

--- a/solution.py
+++ b/solution.py
@@ -13,7 +13,7 @@
 AXES = ("comm", "sub")
 
 
-def build_rows(index_ref, count_ref, importance_ref, own_ref, halo_ref, first, *, rows, halo):
+def build_rows(index_ref, count_ref, importance_ref, own_ref, halo_ref, first, target, *, rows, halo):
     his = (rows + halo + 255) // 256
     pairs = (his + 1) // 2
     fanout = index_ref.shape[0]
@@ -72,7 +72,7 @@
             tile = jnp.concatenate([t[h * 8 : (h + 1) * 8, :] for t in tiles], axis=0).astype(BF)
             to = slice(first + g, first + g + 16)
             if h * 256 < rows:
-                own_ref[to, h * 256 : (h + 1) * 256] = tile
+                own_ref[pl.ds(pl.multiple_of(target + g, 16), 16), h * 256 : (h + 1) * 256] = tile
             else:
                 start = h * 256 - rows
                 stop = min(start + 256, halo)
@@ -81,7 +81,7 @@
 
 def build_kernel(index_ref, count_ref, importance_ref, own_ref, halo_ref, *, rows, halo):
     for first in range(0, own_ref.shape[0], 128):
-        build_rows(index_ref, count_ref, importance_ref, own_ref, halo_ref, first, rows=rows, halo=halo)
+        build_rows(index_ref, count_ref, importance_ref, own_ref, halo_ref, first, first, rows=rows, halo=halo)
 
 
 def build_mixing(nbr_index, nbr_count, importance, halo):
@@ -119,16 +119,56 @@
 
 def hidden_rows(features_ref, q, bias, sent_rows, low_ref, neigh_ref, slope_ref, sent_ref, start):
     block, width = features_ref.shape
+    at_rows = pl.ds(pl.multiple_of(start, block), block)
     low_ref[...] = features_ref[...].astype(BF)
     for c in range(0, width, 256):
-        pre = jnp.dot(low_ref[...], q[:, c : c + 256], preferred_element_type=F32) + bias[:, c : c + 256]
+        at = slice(c, c + 256)
+        pre = jnp.dot(low_ref[...], q[:, at], preferred_element_type=F32) + bias[:, at]
         value, slope = gelu_pair(pre)
-        neigh_ref[:, c : c + 256] = value.astype(BF)
-        slope_ref[:, c : c + 256] = slope.astype(BF)
+        neigh_ref[at_rows, at] = value.astype(BF)
+        slope_ref[:, at] = slope.astype(BF)
     local = lax.broadcasted_iota(jnp.int32, (sent_rows.shape[0], block), 1) + start
     chosen = jnp.where(local == sent_rows, 1.0, 0.0).astype(BF)
-    picked = jnp.dot(chosen, neigh_ref[...], preferred_element_type=F32)
-    sent_ref[...] += picked
+    sent_ref[...] += jnp.dot(chosen, neigh_ref[at_rows, :], preferred_element_type=F32)
+
+
+def ring_copies(groups, index, blocks_ref, landed_ref, send_sem, recv_sem, device_of):
+    copies = []
+    for k in range(1, groups):
+        other = (index + k) % groups
+        copies.append(
+            pltpu.make_async_remote_copy(
+                src_ref=blocks_ref.at[other],
+                dst_ref=landed_ref.at[index],
+                send_sem=send_sem.at[k - 1],
+                recv_sem=recv_sem.at[k - 1],
+                device_id=device_of(other),
+                device_id_type=pl.DeviceIdType.MESH,
+            )
+        )
+    return copies
+
+
+def regroup(x, outer, inner, per):
+    count = x.shape[0]
+    to = lax.broadcasted_iota(jnp.int32, (count, count), 0)
+    place = lax.broadcasted_iota(jnp.int32, (count, count), 1)
+    source = ((to // per) % outer) * (inner * per) + (to // (per * outer)) * per + to % per
+    chosen = jnp.where(place == source, 1.0, 0.0).astype(BF)
+    return jnp.dot(chosen, x, preferred_element_type=F32).astype(BF)
+
+
+def greet(comm, sub, comms, subs):
+    barrier = pltpu.get_barrier_semaphore()
+    for k in range(1, comms):
+        pl.semaphore_signal(
+            barrier, inc=1, device_id=((comm + k) % comms, sub), device_id_type=pl.DeviceIdType.MESH
+        )
+    for k in range(1, subs):
+        pl.semaphore_signal(
+            barrier, inc=1, device_id=(comm, (sub + k) % subs), device_id_type=pl.DeviceIdType.MESH
+        )
+    pl.semaphore_wait(barrier, comms + subs - 2)
 
 
 def gather_kernel(
@@ -140,33 +180,49 @@
     w_ref,
     bias_ref,
     send_ref,
-    own_ref,
+    own_out,
     halo_ref,
     low_ref,
-    neigh_ref,
     slope_ref,
-    sent_ref,
+    pooled_ref,
+    incoming_ref,
     q_full,
     w_full,
     bias_out,
+    own_mix,
+    neigh,
     q_buf,
     w_own,
     bias_buf,
     sent_acc,
+    sub_blocks,
+    sub_landed,
+    comm_blocks,
+    comm_landed,
     local_sem,
+    mix_sem,
     send_sem,
     recv_sem,
+    sub_send,
+    sub_recv,
+    comm_send,
+    comm_recv,
     *,
+    comms,
     subs,
     bits,
+    block,
+    pool_block,
 ):
     i = pl.program_id(0)
-    rows = own_ref.shape[1]
+    rows = own_mix.shape[0]
     halo = halo_ref.shape[1]
-    builds = rows // own_ref.shape[0]
-    block, width = features_ref.shape
-    steps = builds + rows // block
-    me = lax.axis_index("comm") * subs + lax.axis_index("sub")
+    width = neigh.shape[1]
+    builds = rows // block
+    hidden_end = 2 * builds
+    steps = hidden_end + rows // pool_block
+    comm, sub = lax.axis_index("comm"), lax.axis_index("sub")
+    me = comm * subs + sub
     mine = [(me // (1 << b)) % 2 for b in range(bits)]
     order = list(range(bits))[::-1]
 
@@ -178,25 +234,22 @@
         lead = tuple(slice(None) if b in done else mine[b] for b in order)
         return lead + (part, columns)
 
-    def copy(n, source, target, b):
+    high = list(range(3, bits))[::-1]
+    left, right = pl.ds(0, width // 2), pl.ds(width // 2, width // 2)
+    count = [0]
+
+    def exchange(buf, b, done, part=slice(None), columns=slice(None), source=None):
+        at = buf.at[spot(done, part, columns)]
+        n = count[0]
+        count[0] += 1
         return pltpu.make_async_remote_copy(
-            src_ref=source,
-            dst_ref=target,
+            src_ref=at if source is None else source,
+            dst_ref=at,
             send_sem=send_sem.at[n],
             recv_sem=recv_sem.at[n],
             device_id=partner(b),
             device_id_type=pl.DeviceIdType.MESH,
         )
-
-    high = list(range(3, bits))[::-1]
-    left, right = pl.ds(0, width // 2), pl.ds(width // 2, width // 2)
-    count = [0]
-
-    def exchange(buf, b, done, part=slice(None), columns=slice(None), source=None):
-        at = buf.at[spot(done, part, columns)]
-        n = count[0]
-        count[0] += 1
-        return copy(n, at if source is None else source, at, b)
 
     def chain(buf, own, split, part=slice(None)):
         groups = []
@@ -222,11 +275,17 @@
         "bias": chain(bias_buf, None, False),
         "w0": chain(w_full, w_own.at[top], True, top),
         "w1": chain(w_full, w_own.at[bottom], True, bottom),
+        "sub": [ring_copies(subs, sub, sub_blocks, sub_landed, sub_send, sub_recv, lambda j: (comm, j))],
+        "comm": [ring_copies(comms, comm, comm_blocks, comm_landed, comm_send, comm_recv, lambda j: (j, sub))],
     }
     w_local = pltpu.make_async_copy(w_own, w_full.at[spot([])], local_sem.at[0])
     q_local = pltpu.make_async_copy(q_buf, q_full, local_sem.at[1])
     last = len(chains["q"]) - 1
 
+    def mix_copy(step):
+        at = pl.ds(pl.multiple_of(step * block, block), block)
+        return pltpu.make_async_copy(own_mix.at[at, :], own_out.at[at, :], mix_sem)
+
     def begin(name, n):
         for c in chains[name][n]:
             c.start()
@@ -235,9 +294,17 @@
         for c in chains[name][n]:
             c.wait()
 
-    def advance(name, n):
-        finish(name, n)
-        begin(name, n + 1)
+    def happen(part):
+        for (step, at), names in events.items():
+            if at == part:
+
+                @pl.when(i == step)
+                def _(names=names):
+                    for name, n in names:
+                        if n >= 0:
+                            finish(name, n)
+                        if n < last:
+                            begin(name, n + 1)
 
     @pl.when(i == 0)
     def _():
@@ -246,10 +313,7 @@
         bias_buf[spot([])] = bias_ref[...]
         sent_acc[...] = jnp.zeros_like(sent_acc)
         w_local.start()
-        barrier = pltpu.get_barrier_semaphore()
-        for b in range(bits):
-            pl.semaphore_signal(barrier, inc=1, device_id=partner(b), device_id_type=pl.DeviceIdType.MESH)
-        pl.semaphore_wait(barrier, bits)
+        greet(comm, sub, comms, subs)
         begin("q", 0)
         begin("bias", 0)
         w_local.wait()
@@ -264,32 +328,34 @@
         (5, 1): [("w1", 0)],
         (7, 0): [("w0", 2), ("w1", 1)],
         (8, 0): [("q", 3), ("bias", 3)],
-        (builds + 1, 0): [("w0", 3)],
-        (builds + 2, 0): [("w1", 2)],
+        (builds + 2, 0): [("w0", 3)],
+        (builds + 4, 0): [("w1", 2)],
+        (hidden_end, 0): [("w0", 4)],
+        (hidden_end + 1, 0): [("w1", 3)],
     }
 
-    def happen(part):
-        for (step, at), names in events.items():
-            if at == part:
-
-                @pl.when(i == step)
-                def _(names=names):
-                    for name, n in names:
-                        if n < 0:
-                            begin(name, 0)
-                        else:
-                            advance(name, n)
-
     happen(0)
-    for part in range(2):
+    for part in range(block // 128):
         if part == 1:
             happen(1)
 
         @pl.when(i < builds)
         def _(part=part):
             build_rows(
-                index_ref, count_ref, importance_ref, own_ref, halo_ref, part * 128, rows=rows, halo=halo
+                index_ref,
+                count_ref,
+                importance_ref,
+                own_mix,
+                halo_ref,
+                part * 128,
+                i * block + part * 128,
+                rows=rows,
+                halo=halo,
             )
+
+    @pl.when(i < builds)
+    def _():
+        mix_copy(i).start()
 
     @pl.when(i == builds)
     def _():
@@ -305,8 +371,9 @@
             bias_out[k : k + 1, :] = jnp.concatenate(pieces, axis=1).astype(BF).astype(F32)
         bias_out[2:, :] = jnp.zeros((6, width), F32)
 
-    @pl.when(i >= builds)
-    def _():
+    @pl.when(jnp.logical_and(i >= builds, i < hidden_end))
+    def _():
+        mix_copy(i - builds).wait()
         q = q_buf[...].reshape(width, width)
         hidden_rows(
             features_ref,
@@ -314,19 +381,37 @@
             bias_out[0:1, :],
             send_ref[...],
             low_ref,
-            neigh_ref,
+            neigh,
             slope_ref,
             sent_acc,
             (i - builds) * block,
         )
 
+    @pl.when(i == hidden_end - 1)
+    def _():
+        sub_blocks[...] = sent_acc[...].astype(BF).reshape(sub_blocks.shape)
+        begin("sub", 0)
+        sub_landed[sub] = sub_blocks[sub]
+
+    @pl.when(i == hidden_end + 2)
+    def _():
+        finish("sub", 0)
+        moved = regroup(sub_landed[...].reshape(halo, width), subs, comms, halo // (subs * comms))
+        comm_blocks[...] = moved.reshape(comm_blocks.shape)
+        begin("comm", 0)
+        comm_landed[comm] = comm_blocks[comm]
+
+    @pl.when(i >= hidden_end)
+    def _():
+        at = pl.ds(pl.multiple_of((i - hidden_end) * pool_block, pool_block), pool_block)
+        pooled_ref[...] = jnp.dot(own_mix[at, :], neigh[...], preferred_element_type=F32)
+
     @pl.when(i == steps - 1)
     def _():
-        sent_ref[...] = sent_acc[...].astype(BF)
-        finish("w0", last)
-        advance("w1", last - 1)
+        finish("w1", last)
         q_local.wait()
-        finish("w1", last)
+        finish("comm", 0)
+        incoming_ref[...] = comm_landed[...].reshape(halo, width)
 
 
 def gather_and_transform(features, q_weight, q_bias, w_weight, w_bias, nbr_index, nbr_count, importance, send_rows):
@@ -335,12 +420,14 @@
     bits = devices.bit_length() - 1
     rows, width = features.shape
     fanout = nbr_index.shape[1]
-    halo = send_rows.shape[1] * send_rows.shape[2]
-    block = 256
+    per = send_rows.shape[2]
+    halo = devices * per
+    block, pool_block = 256, 384
     builds = rows // block
     q_rows, w_rows = q_weight.shape[0], w_weight.shape[0]
     share = q_bias.shape[0]
     bias_tile = jnp.pad(jnp.concatenate([q_bias, w_bias])[None], ((0, 7), (0, 128 - 2 * share)))
+    by_sub = send_rows.reshape(comms, subs, per).transpose(1, 0, 2).reshape(halo, 1)
     lead = (2,) * bits
 
     def built(i):
@@ -350,15 +437,20 @@
         return (0, jnp.minimum(i, builds - 1))
 
     def later(i):
-        return (jnp.maximum(i - builds, 0), 0)
+        return (jnp.clip(i - builds, 0, builds - 1), 0)
+
+    def pooled_at(i):
+        return (jnp.maximum(i - 2 * builds, 0), 0)
 
     def whole(*shape):
         return pl.BlockSpec(shape, lambda i: (0,) * len(shape))
 
     copies = 4 * bits + 3 * 2
     out = pl.pallas_call(
-        functools.partial(gather_kernel, subs=subs, bits=bits),
-        grid=(builds + rows // block,),
+        functools.partial(
+            gather_kernel, comms=comms, subs=subs, bits=bits, block=block, pool_block=pool_block
+        ),
+        grid=(2 * builds + rows // pool_block,),
         in_specs=[
             pl.BlockSpec((fanout, block), built_columns),
             pl.BlockSpec((1, block), built_columns),
@@ -370,11 +462,11 @@
             whole(halo, 1),
         ],
         out_specs=[
-            pl.BlockSpec((block, rows), built),
+            pl.BlockSpec(memory_space=pl.ANY),
             pl.BlockSpec((block, halo), built),
             pl.BlockSpec((block, width), later),
             pl.BlockSpec((block, width), later),
-            pl.BlockSpec((block, width), later),
+            pl.BlockSpec((pool_block, width), pooled_at),
             whole(halo, width),
             pl.BlockSpec(memory_space=pl.ANY),
             pl.BlockSpec(memory_space=pl.ANY),
@@ -385,23 +477,34 @@
             jax.ShapeDtypeStruct((rows, halo), BF),
             jax.ShapeDtypeStruct((rows, width), BF),
             jax.ShapeDtypeStruct((rows, width), BF),
-            jax.ShapeDtypeStruct((rows, width), BF),
+            jax.ShapeDtypeStruct((rows, width), F32),
             jax.ShapeDtypeStruct((halo, width), BF),
             jax.ShapeDtypeStruct(lead + (q_rows, width), BF),
             jax.ShapeDtypeStruct(lead + (w_rows, width), BF),
             jax.ShapeDtypeStruct((8, width), F32),
         ],
         scratch_shapes=[
+            pltpu.VMEM((rows, rows), BF),
+            pltpu.VMEM((rows, width), BF),
             pltpu.VMEM(lead + (q_rows, width), BF),
             pltpu.VMEM((w_rows, width), BF),
             pltpu.VMEM(lead + (8, 128), F32),
             pltpu.VMEM((halo, width), F32),
+            pltpu.VMEM((subs, halo // subs, width), BF),
+            pltpu.VMEM((subs, halo // subs, width), BF),
+            pltpu.VMEM((comms, halo // comms, width), BF),
+            pltpu.VMEM((comms, halo // comms, width), BF),
             pltpu.SemaphoreType.DMA((2,)),
+            pltpu.SemaphoreType.DMA,
             pltpu.SemaphoreType.DMA((copies,)),
             pltpu.SemaphoreType.DMA((copies,)),
+            pltpu.SemaphoreType.DMA((subs - 1,)),
+            pltpu.SemaphoreType.DMA((subs - 1,)),
+            pltpu.SemaphoreType.DMA((comms - 1,)),
+            pltpu.SemaphoreType.DMA((comms - 1,)),
         ],
         compiler_params=pltpu.CompilerParams(
-            collective_id=0, has_side_effects=True, vmem_limit_bytes=48 * 2**20
+            collective_id=0, has_side_effects=True, vmem_limit_bytes=56 * 2**20
         ),
         name="gather_and_transform",
     )(
@@ -412,16 +515,16 @@
         q_weight,
         w_weight,
         bias_tile,
-        send_rows.reshape(halo, 1),
+        by_sub,
     )
-    own_mix, halo_mix, low, neigh, slope, sent, q_full, w_full, biases = out
+    own_mix, halo_mix, low, slope, pooled_own, incoming, q_full, w_full, biases = out
     return (
         own_mix,
         halo_mix,
         low,
-        neigh,
         slope,
-        sent,
+        pooled_own,
+        incoming,
         q_full.reshape(devices * q_rows, width),
         w_full.reshape(devices * w_rows, width),
         biases[0],
@@ -442,8 +545,10 @@
     low = features.astype(BF)
     neigh, slope = gelu_pair(jnp.dot(low, q_full, preferred_element_type=F32) + qbias_full)
     neigh = neigh.astype(BF)
-    sent = neigh[send_rows.reshape(-1)]
-    return own_mix, halo_mix, low, neigh, slope.astype(BF), sent, q_full, w_full, qbias_full, wbias_full
+    sent = neigh[send_rows[0]]
+    incoming = lax.all_to_all(sent, AXES, split_axis=0, concat_axis=0, tiled=True).reshape(halo, width)
+    pooled_own = pool_own(own_mix, neigh)
+    return own_mix, halo_mix, low, slope.astype(BF), pooled_own, incoming, q_full, w_full, qbias_full, wbias_full
 
 
 def resident(*shape):
@@ -626,6 +731,496 @@
     return jnp.concatenate([h[0] for h in halves], axis=0)
 
 
+def back_plain(
+    own_mix, low, slope, pooled, grad_out, grad_pooled, sent_grad, grad_wbias, q_full, w_full, send_rows
+):
+    rows, width = low.shape
+    devices, per = send_rows.shape[1:]
+    contract = (((0,), (0,)), ((), ()))
+    returned = lax.all_to_all(
+        sent_grad.reshape(devices, per, width), AXES, split_axis=0, concat_axis=0, tiled=True
+    )
+    joined = jnp.concatenate([low, pooled], axis=1)
+    grad_w = lax.dot_general(joined, grad_out, contract, preferred_element_type=F32)
+    grad_low = lax.dot_general(grad_out, w_full[:width], (((1,), (1,)), ((), ())), preferred_element_type=F32)
+    grad_neigh = lax.dot_general(own_mix, grad_pooled, contract, preferred_element_type=F32)
+    grad_neigh = grad_neigh.at[send_rows.reshape(-1)].add(returned.reshape(devices * per, width))
+    grad_hidden = (slope.astype(F32) * grad_neigh).astype(BF)
+    grad_q = lax.dot_general(low, grad_hidden, contract, preferred_element_type=F32)
+    grad_qbias = jnp.sum(grad_hidden.astype(F32), axis=0)
+    grad_features = grad_low + lax.dot_general(
+        grad_hidden, q_full, (((1,), (1,)), ((), ())), preferred_element_type=F32
+    )
+    me = lax.axis_index(AXES)
+    share = width // devices
+    sums = summed(jnp.stack([grad_qbias, grad_wbias[0]]), devices)
+    sums = lax.dynamic_slice_in_dim(sums, me * share, share, 1)
+    return (
+        grad_features,
+        scatter_sum(grad_q.astype(BF), devices),
+        sums[0],
+        scatter_sum(grad_w.astype(BF), devices),
+        sums[1],
+    )
+
+
+class ScatterSum:
+    def __init__(self, refs, orders, mine, partner):
+        self.held, self.sent, self.got, self.next_sent, self.next_got, self.send_sem, self.recv_sem = refs
+        self.orders, self.mine, self.partner = orders, mine, partner
+        self.bits = len(mine)
+        self.lead = list(range(1, self.bits))[::-1]
+        self.half = self.held.shape[-1] // 2
+
+    def copy(self, n, source, target, b):
+        return pltpu.make_async_remote_copy(
+            src_ref=source,
+            dst_ref=target,
+            send_sem=self.send_sem.at[n],
+            recv_sem=self.recv_sem.at[n],
+            device_id=self.partner(b),
+            device_id_type=pl.DeviceIdType.MESH,
+        )
+
+    def first(self, top):
+        return self.copy(top, self.sent.at[self.top_index(top)], self.got.at[self.top_index(top)], 0)
+
+    def top_index(self, top):
+        return ((top // 2) % 2, top % 2)
+
+    def later(self, k):
+        out = []
+        for h in range(2):
+            n = 4 + 2 * (k - 1) + h
+            at = (h,) + (slice(self.offset(k), self.offset(k) + (1 << (self.bits - 1 - k))),)
+            out.append(self.copy(n, self.next_sent.at[at], self.next_got.at[at], self.orders[h][k - 1]))
+        return out
+
+    def offset(self, k):
+        return (1 << (self.bits - 1)) - (1 << (self.bits - k))
+
+    def spot(self, chosen):
+        return tuple(chosen[b] for b in self.lead)
+
+    def absorb(self, k):
+        for h in range(2):
+            order = self.orders[h]
+            fixed = order[:k]
+            free = [b for b in self.lead if b not in fixed]
+            columns = slice(h * self.half, (h + 1) * self.half)
+
+            def total(chosen, h=h, free=free, columns=columns):
+                at = self.spot(chosen)
+                if k == 0:
+                    came = self.got[at + (slice(None), columns)]
+                else:
+                    place = self.offset(k)
+                    for p, b in enumerate(free[::-1]):
+                        place = place + chosen[b] * (1 << p)
+                    came = self.next_got[h, place]
+                return at, self.held[at + (slice(None), columns)] + came.astype(F32)
+
+            if not free:
+                at, value = total({b: self.mine[b] for b in fixed})
+                self.held[at + (slice(None), columns)] = value
+                continue
+            split = order[k]
+            others = [b for b in free if b != split]
+
+            def body(n, carry, total=total, split=split, others=others, fixed=fixed, columns=columns, h=h):
+                chosen = {b: self.mine[b] for b in fixed}
+                for p, b in enumerate(others[::-1]):
+                    chosen[b] = (n // (1 << p)) % 2
+                chosen[split] = self.mine[split]
+                at, value = total(chosen)
+                self.held[at + (slice(None), columns)] = value
+                chosen[split] = 1 - self.mine[split]
+                _, value = total(chosen)
+                self.next_sent[h, self.offset(k + 1) + n] = value.astype(BF)
+                return carry
+
+            lax.fori_loop(0, 1 << len(others), body, 0)
+
+    def start(self, k):
+        for c in self.later(k):
+            c.start()
+
+    def wait(self, k):
+        for c in [self.first(t) for t in range(4)] if k == 0 else self.later(k):
+            c.wait()
+
+    def result(self):
+        return self.held[self.spot({b: self.mine[b] for b in self.lead})]
+
+
+def back_body(
+    mix_ref,
+    slope_ref,
+    sent_grad_ref,
+    w_bias_ref,
+    target_ref,
+    low_hbm,
+    pooled_hbm,
+    out_hbm,
+    grad_pooled_hbm,
+    w_hbm,
+    q_hbm,
+    features_ref,
+    q_out,
+    w_out,
+    bias_out,
+    joined,
+    grad_out,
+    grad_pooled,
+    w_top,
+    q_full,
+    q_bias_acc,
+    bias_sent,
+    bias_got,
+    comm_blocks,
+    comm_landed,
+    sub_blocks,
+    sub_landed,
+    *rest,
+    comms,
+    subs,
+    bits,
+    mix_block,
+    row_block,
+):
+    sets = [rest[7 * k : 7 * k + 7] for k in range(3)]
+    load_sem, bias_send, bias_recv, comm_send, comm_recv, sub_send, sub_recv = rest[21:]
+    i = pl.program_id(0)
+    rows, width = grad_out.shape
+    halo = sent_grad_ref.shape[0]
+    half = width // 2
+    comm, sub = lax.axis_index("comm"), lax.axis_index("sub")
+    me = comm * subs + sub
+    mine = [(me // (1 << b)) % 2 for b in range(bits)]
+    tn = (((0,), (0,)), ((), ()))
+    nt = (((1,), (1,)), ((), ()))
+
+    def partner(b):
+        other = me + (1 << b) * (1 - 2 * mine[b])
+        return (other // subs, other % subs)
+
+    high = list(range(3, bits))
+    orders = ([1, 2] + high, [2, 1] + high)
+    w_sets = [ScatterSum(sets[k], orders, mine, partner) for k in range(2)]
+    q_set = ScatterSum(sets[2], orders, mine, partner)
+
+    left, right = pl.ds(0, half), pl.ds(half, half)
+    loads = [
+        (out_hbm.at[:, left], grad_out.at[:, left]),
+        (low_hbm.at[:, left], joined.at[:, pl.ds(0, half)]),
+        (low_hbm.at[:, right], joined.at[:, pl.ds(half, half)]),
+        (pooled_hbm.at[:, left], joined.at[:, pl.ds(2 * half, half)]),
+        (pooled_hbm.at[:, right], joined.at[:, pl.ds(3 * half, half)]),
+        (out_hbm.at[:, right], grad_out.at[:, right]),
+        (grad_pooled_hbm, grad_pooled),
+        (w_hbm.at[pl.ds(0, width), :], w_top),
+        (q_hbm, q_full),
+    ]
+    loads = [pltpu.make_async_copy(a, b, load_sem.at[n]) for n, (a, b) in enumerate(loads)]
+    comm_ring = ring_copies(comms, comm, comm_blocks, comm_landed, comm_send, comm_recv, lambda j: (j, sub))
+    sub_ring = ring_copies(subs, sub, sub_blocks, sub_landed, sub_send, sub_recv, lambda j: (comm, j))
+    bias_copies = [
+        pltpu.make_async_remote_copy(
+            src_ref=bias_sent.at[b],
+            dst_ref=bias_got.at[b],
+            send_sem=bias_send.at[b],
+            recv_sem=bias_recv.at[b],
+            device_id=partner(b),
+            device_id_type=pl.DeviceIdType.MESH,
+        )
+        for b in range(bits)
+    ]
+
+    products = 8
+    spreads = rows // mix_block
+    spread_end = products + spreads
+    q_end = spread_end + 4
+    steps = q_end + rows // row_block
+
+    def load_wait(step, which):
+        @pl.when(i == step)
+        def _():
+            for n in which:
+                loads[n].wait()
+
+    @pl.when(i == 0)
+    def _():
+        for c in loads:
+            c.start()
+        greet(comm, sub, comms, subs)
+        comm_blocks[...] = sent_grad_ref[...].astype(BF).reshape(comm_blocks.shape)
+        for c in comm_ring:
+            c.start()
+        comm_landed[comm] = comm_blocks[comm]
+        q_bias_acc[...] = jnp.zeros_like(q_bias_acc)
+
+    load_wait(0, [0, 1])
+    load_wait(1, [2])
+    load_wait(2, [3])
+    load_wait(3, [4])
+    load_wait(4, [5])
+    load_wait(products, [6])
+    load_wait(q_end, [7, 8])
+
+    @pl.when(i == 2)
+    def _():
+        for c in comm_ring:
+            c.wait()
+        moved = regroup(comm_landed[...].reshape(halo, width), comms, subs, halo // (subs * comms))
+        sub_blocks[...] = moved.reshape(sub_blocks.shape)
+        for c in sub_ring:
+            c.start()
+        sub_landed[sub] = sub_blocks[sub]
+
+    def step_of(which, k):
+        which.wait(k)
+        which.absorb(k)
+        if k < bits - 1:
+            which.start(k + 1)
+
+    def deal(value, which, top, rows_each):
+        keep_even = mine[0] == 0
+        shares = value.shape[0] // rows_each
+        for p in range(shares // 2):
+            even = value[2 * p * rows_each : (2 * p + 1) * rows_each]
+            odd = value[(2 * p + 1) * rows_each : (2 * p + 2) * rows_each]
+            at = top + tuple((p >> b) & 1 for b in range(bits - 2, -1, -1))[len(top) :]
+            which.held[at] = jnp.where(keep_even, even, odd)
+            which.sent[at] = jnp.where(keep_even, odd, even).astype(BF)
+
+    def w_top_bits(j):
+        return ((j // 2) % 2, j % 2)
+
+    for n in range(2):
+
+        @pl.when(jnp.logical_and(i >= 4 * n, i < 4 * n + 4))
+        def _(n=n):
+            j = i - 4 * n
+            at = pl.ds(pl.multiple_of(j * half, half), half)
+            columns = slice(n * half, (n + 1) * half)
+            value = lax.dot_general(joined[:, at], grad_out[:, columns], tn, preferred_element_type=F32)
+            deal(value, w_sets[n], w_top_bits(j), w_out.shape[0])
+            for t in range(4):
+
+                @pl.when(j == t)
+                def _(t=t):
+                    w_sets[n].first(t).start()
+
+    events = {
+        5: [(0, 0)],
+        products + 1: [(1, 0), (0, 1)],
+        products + 3: [(0, 2)],
+        products + 4: [(1, 1)],
+        products + 5: [(0, 3)],
+        spread_end + 1: [(1, 2), (0, 4)],
+        spread_end + 3: [(1, 3)],
+        q_end + 1: [(1, 4)],
+    }
+    for step, which in events.items():
+
+        @pl.when(i == step)
+        def _(which=which):
+            for n, k in which:
+                step_of(w_sets[n], k)
+
+    @pl.when(i == products)
+    def _():
+        for c in sub_ring:
+            c.wait()
+
+    @pl.when(jnp.logical_and(i >= products, i < spread_end))
+    def _():
+        start = (i - products) * mix_block
+        local = lax.broadcasted_iota(jnp.int32, (mix_block, halo), 0) + start
+        chosen = jnp.where(local == target_ref[...], 1.0, 0.0).astype(BF)
+        back = lax.dot_general(mix_ref[...], grad_pooled[...], tn, preferred_element_type=F32)
+        back += jnp.dot(chosen, sub_landed[...].reshape(halo, width), preferred_element_type=F32)
+        grad = (back * slope_ref[...].astype(F32)).astype(BF)
+        joined[pl.ds(pl.multiple_of(start, 128), mix_block), width:] = grad
+        q_bias_acc[0:1, :] += jnp.sum(grad.astype(F32), axis=0, keepdims=True)
+
+    @pl.when(jnp.logical_and(i >= spread_end, i < q_end))
+    def _():
+        for t in range(4):
+
+            @pl.when(i == spread_end + t)
+            def _(t=t):
+                n, j = t % 2, t // 2
+                value = lax.dot_general(
+                    joined[:, j * half : (j + 1) * half],
+                    joined[:, width + n * half : width + (n + 1) * half],
+                    tn,
+                    preferred_element_type=F32,
+                )
+                keep_even = mine[0] == 0
+                columns = slice(n * half, (n + 1) * half)
+                each = q_out.shape[0]
+                for p in range(half // each // 2):
+                    even = value[2 * p * each : (2 * p + 1) * each]
+                    odd = value[(2 * p + 1) * each : (2 * p + 2) * each]
+                    at = (j, (p >> 2) & 1, (p >> 1) & 1, p & 1, slice(None), columns)
+                    q_set.held[at] = jnp.where(keep_even, even, odd)
+                    q_set.sent[at] = jnp.where(keep_even, odd, even).astype(BF)
+                if n == 1:
+                    q_set.first(2 * j).start()
+                    q_set.first(2 * j + 1).start()
+
+    def bias_step(b):
+        if b:
+            bias_copies[b - 1].wait()
+            total = bias_sent[b - 1] + bias_got[b - 1]
+            if b == bits:
+                bias_out[...] = total
+                return
+            bias_sent[b] = total
+        bias_copies[b].start()
+
+    @pl.when(i == spread_end)
+    def _():
+        pieces = [w_bias_ref[0:1, c : c + 128] for c in range(0, width, 128)]
+        pieces += [q_bias_acc[0:1, c : c + 128] for c in range(0, width, 128)]
+        bias_sent[0] = jnp.concatenate(pieces, axis=0)
+
+    for b in range(bits):
+
+        @pl.when(i == spread_end + b)
+        def _(b=b):
+            bias_step(b)
+
+    q_events = {q_end + 1: 0, q_end + 4: 1}
+    for step, k in q_events.items():
+
+        @pl.when(i == step)
+        def _(k=k):
+            step_of(q_set, k)
+
+    @pl.when(i >= q_end)
+    def _():
+        at = pl.ds(pl.multiple_of((i - q_end) * row_block, 128), row_block)
+        value = lax.dot_general(grad_out[at, :], w_top[...], nt, preferred_element_type=F32)
+        features_ref[...] = value + lax.dot_general(
+            joined[at, width:], q_full[...], nt, preferred_element_type=F32
+        )
+
+    @pl.when(i == steps - 1)
+    def _():
+        for k in range(2, bits):
+            step_of(q_set, k)
+        for n in range(2):
+            w_out[:, n * half : (n + 1) * half] = w_sets[n].result()
+        q_out[...] = q_set.result()
+        bias_step(bits)
+
+
+def back_kernel(
+    own_mix, low, slope, pooled, grad_out, grad_pooled, sent_grad, grad_wbias, q_full, w_full, send_rows
+):
+    comms, subs = lax.axis_size("comm"), lax.axis_size("sub")
+    devices = comms * subs
+    bits = devices.bit_length() - 1
+    rows, width = low.shape
+    per = send_rows.shape[2]
+    halo = devices * per
+    mix_block, row_block = 384, 384
+    spreads = rows // mix_block
+    spread_end = 8 + spreads
+    q_end = spread_end + 4
+    w_rows, q_rows = w_full.shape[0] // devices, q_full.shape[0] // devices
+    targets = send_rows.reshape(comms, subs, per).transpose(1, 0, 2).reshape(1, halo)
+    lead = (2,) * (bits - 1)
+
+    def set_scratch(rows_each, columns):
+        chunks = (1 << (bits - 1)) - 1
+        copies = 4 + 2 * (bits - 1)
+        return [
+            pltpu.VMEM(lead + (rows_each, columns), F32),
+            pltpu.VMEM(lead + (rows_each, columns), BF),
+            pltpu.VMEM(lead + (rows_each, columns), BF),
+            pltpu.VMEM((2, chunks, rows_each, columns // 2), BF),
+            pltpu.VMEM((2, chunks, rows_each, columns // 2), BF),
+            pltpu.SemaphoreType.DMA((copies,)),
+            pltpu.SemaphoreType.DMA((copies,)),
+        ]
+
+    def spread_columns(i):
+        return (0, jnp.clip(i - 8, 0, spreads - 1))
+
+    def spread_rows(i):
+        return (jnp.clip(i - 8, 0, spreads - 1), 0)
+
+    def whole(*shape):
+        return pl.BlockSpec(shape, lambda i: (0,) * len(shape), pipeline_mode=pl.Buffered(1))
+
+    def whole_out(*shape):
+        return pl.BlockSpec(shape, lambda i: (0,) * len(shape))
+
+    anywhere = pl.BlockSpec(memory_space=pl.ANY)
+    grad_features, grad_q, grad_w, biases = pl.pallas_call(
+        functools.partial(
+            back_body, comms=comms, subs=subs, bits=bits, mix_block=mix_block, row_block=row_block
+        ),
+        grid=(q_end + rows // row_block,),
+        in_specs=[
+            pl.BlockSpec((rows, mix_block), spread_columns),
+            pl.BlockSpec((mix_block, width), spread_rows),
+            whole(halo, width),
+            whole(8, width),
+            whole(1, halo),
+        ]
+        + [anywhere] * 6,
+        out_specs=[
+            pl.BlockSpec((row_block, width), lambda i: (jnp.maximum(i - q_end, 0), 0)),
+            whole_out(q_rows, width),
+            whole_out(w_rows, width),
+            whole_out(16, 128),
+        ],
+        out_shape=[
+            jax.ShapeDtypeStruct((rows, width), F32),
+            jax.ShapeDtypeStruct((q_rows, width), F32),
+            jax.ShapeDtypeStruct((w_rows, width), F32),
+            jax.ShapeDtypeStruct((16, 128), F32),
+        ],
+        scratch_shapes=[
+            pltpu.VMEM((rows, 2 * width), BF),
+            pltpu.VMEM((rows, width), BF),
+            pltpu.VMEM((rows, width), BF),
+            pltpu.VMEM((width, width), BF),
+            pltpu.VMEM((width, width), BF),
+            pltpu.VMEM((8, width), F32),
+            pltpu.VMEM((bits, 16, 128), F32),
+            pltpu.VMEM((bits, 16, 128), F32),
+            pltpu.VMEM((comms, halo // comms, width), BF),
+            pltpu.VMEM((comms, halo // comms, width), BF),
+            pltpu.VMEM((subs, halo // subs, width), BF),
+            pltpu.VMEM((subs, halo // subs, width), BF),
+        ]
+        + set_scratch(w_rows, width // 2)
+        + set_scratch(w_rows, width // 2)
+        + set_scratch(q_rows, width)
+        + [
+            pltpu.SemaphoreType.DMA((9,)),
+            pltpu.SemaphoreType.DMA((bits,)),
+            pltpu.SemaphoreType.DMA((bits,)),
+            pltpu.SemaphoreType.DMA((comms - 1,)),
+            pltpu.SemaphoreType.DMA((comms - 1,)),
+            pltpu.SemaphoreType.DMA((subs - 1,)),
+            pltpu.SemaphoreType.DMA((subs - 1,)),
+        ],
+        compiler_params=pltpu.CompilerParams(
+            collective_id=1, has_side_effects=True, vmem_limit_bytes=62 * 2**20
+        ),
+        name="back",
+    )(own_mix, slope, sent_grad, grad_wbias, targets, low, pooled, grad_out, grad_pooled, w_full, q_full)
+    share = width // devices
+    sums = lax.dynamic_slice_in_dim(biases.reshape(2, width), lax.axis_index(AXES) * share, share, 1)
+    return grad_features, grad_q, sums[1], grad_w, sums[0]
+
+
 def shards(
     features,
     q_weight,
@@ -638,62 +1233,19 @@
     send_rows,
     cotangent,
 ):
-    devices = lax.axis_size(("comm", "sub"))
-    rows, width = features.shape
-    fanout = nbr_index.shape[1]
-    per_peer = send_rows.shape[2]
-    halo = devices * per_peer
+    devices = lax.axis_size(AXES)
     kernel_fits = devices == 32 and q_weight.shape[0] % 16 == 0
-    gather = gather_and_transform if kernel_fits else gather_plain
-    own_mix, halo_mix, feat_low, neigh_low, slope, outgoing, q_full, w_full, qbias_full, wbias_full = gather(
+    gather, back = (gather_and_transform, back_kernel) if kernel_fits else (gather_plain, back_plain)
+    own_mix, halo_mix, low, slope, pooled_own, incoming, q_full, w_full, qbias_full, wbias_full = gather(
         features, q_weight, q_bias, w_weight, w_bias, nbr_index, nbr_count, importance, send_rows
     )
-    targets = send_rows[0]
-    incoming = lax.all_to_all(
-        outgoing.reshape(devices, per_peer, width), AXES, split_axis=0, concat_axis=0, tiled=True
+    embedding, pooled, grad_out, grad_pooled, sent_grad, grad_wbias = combine(
+        pooled_own, halo_mix, incoming, low, w_full, wbias_full, cotangent
     )
-    pooled_own = pool_own(own_mix, neigh_low)
-    embedding, pooled, grad_pre_out, grad_pooled, outgoing_grad, grad_wbias = combine(
-        pooled_own, halo_mix, incoming.reshape(halo, width), feat_low, w_full, wbias_full, cotangent
+    grad_features, grad_q, grad_qbias, grad_w, grad_wbias = back(
+        own_mix, low, slope, pooled, grad_out, grad_pooled, sent_grad, grad_wbias, q_full, w_full, send_rows
     )
-    grad_wbias = grad_wbias[0]
-    joined = jnp.concatenate([feat_low, pooled], axis=1)
-    contract = (((0,), (0,)), ((), ()))
-    grad_w = lax.dot_general(joined, grad_pre_out, contract, preferred_element_type=F32)
-    grad_low = lax.dot_general(
-        grad_pre_out, w_full[:width], (((1,), (1,)), ((), ())), preferred_element_type=F32
-    )
-    returned = lax.all_to_all(
-        outgoing_grad.reshape(devices, per_peer, width),
-        ("comm", "sub"),
-        split_axis=0,
-        concat_axis=0,
-        tiled=True,
-    )
-    grad_neigh = lax.dot_general(own_mix, grad_pooled, contract, preferred_element_type=F32)
-    grad_neigh = grad_neigh.at[targets.reshape(-1)].add(returned.reshape(halo, width))
-    grad_pre_hidden = (slope.astype(F32) * grad_neigh).astype(BF)
-    grad_q = lax.dot_general(
-        feat_low, grad_pre_hidden, (((0,), (0,)), ((), ())), preferred_element_type=jnp.float32
-    )
-    grad_qbias = jnp.sum(grad_pre_hidden.astype(jnp.float32), axis=0)
-    grad_features = grad_low + lax.dot_general(
-        grad_pre_hidden, q_full, (((1,), (1,)), ((), ())), preferred_element_type=jnp.float32
-    )
-    me = lax.axis_index(AXES)
-    bias_sums = summed(jnp.stack([grad_qbias, grad_wbias]), devices)
-    bias_shards = lax.dynamic_slice_in_dim(bias_sums, me * (width // devices), width // devices, 1)
-    grad_q_shard = scatter_sum(grad_q.astype(BF), devices)
-    grad_w_shard = scatter_sum(grad_w.astype(BF), devices)
-    grad_qbias_shard, grad_wbias_shard = bias_shards[0], bias_shards[1]
-    return (
-        embedding,
-        grad_features,
-        grad_q_shard,
-        grad_qbias_shard,
-        grad_w_shard,
-        grad_wbias_shard,
-    )
+    return embedding, grad_features, grad_q, grad_qbias, grad_w, grad_wbias
 
 
 def solution(mesh):

time: 273 us -> 205 us (0.75)
  Pallas kernels: 101 us -> 181 us
  matrix products: 58.2 us -> 0 us
  starting transfers between devices: 34.1 us -> 0 us
  waiting for transfers between devices: 33.7 us -> 0 us
  other arithmetic: 20.7 us -> 0.75 us
    pallas_call x2, Pallas kernels: 71.3 us -> 151 us  [the longest x1 78.4 us: back_kernel(): pl.pallas_call(functools.partial(back_body, comms=comms, subs=subs, bits=...]
    dot_general x5 -> x0, matrix products: 58.2 us -> none  [the longest x1 16.7 us: shards(): lax.dot_general(own_mix, grad_pooled, contract, preferred_element_type=F32)]
    ppermute x23 -> x0, waiting for transfers between devices: 33.7 us -> none  [swap(): return lax.ppermute(x, AXES, [(i, i ^ 1 << bit) for i in range(devices)])]
    ppermute x23 -> x0, starting transfers between devices: 24.8 us -> none  [swap(): return lax.ppermute(x, AXES, [(i, i ^ 1 << bit) for i in range(devices)])]
    all_to_all x2 -> x0, starting transfers between devices: 9.37 us -> none  [the longest x1 6.01 us: shards(): lax.all_to_all(outgoing_grad.reshape(devices, per_peer, width), ('comm',...]
    scatter-add x1 -> x0, other arithmetic: 8.98 us -> none  [shards(): grad_neigh.at[targets.reshape(-1)].add(returned.reshape(halo, width))]
    reduce_sum x1 -> x0, other arithmetic: 7.03 us -> none  [shards(): grad_qbias = jnp.sum(grad_pre_hidden.astype(jnp.float32), axis=0)]
    unnamed x21 -> x17, local copies, waits for them, and re-layouts: 13 us -> 16.4 us
  transfers between devices with their start and end apart: 25 -> 0, of which waited for: 13 -> 0; matrix products, arithmetic and copies ran while one was open for 19% -> 0% of each run, Pallas kernels for 5% -> 0%
where the time goes in v1:
time: 205 us
  Pallas kernels  181 us (88%)
  local copies, waits for them, and re-layouts  22.6 us (11%)
    pallas_call x1, Pallas kernels, back_kernel(): pl.pallas_call(functools.partial(back_body, comms=comms, subs=subs, bits=...  78.4 us
    pallas_call x1, Pallas kernels, gather_and_transform(): pl.pallas_call(functools.partial(gather_kernel, comms=comms, subs=subs, b...  72.2 us
    pallas_call x1, Pallas kernels, combine(): pl.pallas_call(combine_kernel, grid=(rows // block,), in_specs=[by_rows(b...  30.3 us
    unnamed x17, local copies, waits for them, and re-layouts  16.4 us

profile of v1, /device:TPU:0, one launch (start us, length us, event | category | flops | bytes accessed | tf_op | source)
XLA Modules:
  0.0 204.9 jit_solution(7041470871413915180)
XLA Ops:
  0.6 0.7 maximum_bitcast_fusion
  1.4 0.6 pad.4.bias_ref
  2.0 1.3 reshape.34.count_ref
  3.3 0.8 reshape.35
  4.1 0.1 copy.19
  4.2 0.6 reshape.38.target_ref
  4.8 0.7 reshape.41.send_ref
  5.5 72.2 %gather_and_transform.1 = (bf16[2304,2304]{1,0:T(8,128)(2,1)}, bf16[2304,128]{1,0:T(8,128)(2,1)}, bf16[2304,1024]{1,0:T(8,128)(2,1)}, bf16[2304,1024]{1,0:T(8,12...) custom-call(s32[50,2304]{1,0:T(8,128)} %bitcast.16, ...), custom_call_target="tpu_custom_call" | custom-call | tf_op jit(solution)/shard_map/gather_and_transform/pallas_call | solution.py:449
  77.7 0.8 slice.9.bias_ref
  78.5 0.0 copy-start
  78.5 2.2 %copy-done = bf16[2,2,2,2,2,64,1024]{6,5,4,3,2,1,0:T(8,128)(2,1)S(1)} copy-done((bf16[2,2,2,2,2,64,1024]{6,5,4,3,2,1,0:T(8,128)(2,1)S(1)}, bf16[2,2,2,2,2,64,1024]{6,5,4,3,2,1,0:T(8,128)(2,1)}, u32[]{:S(2)}) %copy-start) | copy-done | bytes 4194328
  80.6 0.0 copy-start.3
  80.6 1.1 copy-done.3
  81.7 0.0 copy-start.4
  81.7 0.9 copy-done.4
  82.7 30.3 %combine.1 = (f32[2304,1024]{1,0:T(8,128)}, bf16[2304,1024]{1,0:T(8,128)(2,1)}, bf16[2304,1024]{1,0:T(8,128)(2,1)}, bf16[2304,1024]{1,0:T(8,128)(2,1)}, f32[128,1024]{1,0:T(8,128)S(1)}, /*index=5*/f32[8,1024]{1,0:T(8,128)S(1)}) custom-call(f32[2304,1024]{1,0:T(8,128)} %get-tuple-element.25.own_ref, bf16[2304,128]{1,0:T(8,128)(2,1)S(1)} %copy-done.3, ...), custom_call_target="tpu_custom_call" | custom-call | flops 14495514624 | bytes 51904512 | tf_op jit(solution)/shard_map/combine/pallas_call | solution.py:652
  112.9 0.0 copy-start.1
  113.0 0.8 copy-done.1
  113.8 0.0 copy-start.2
  113.8 0.6 copy-done.2
  114.4 78.4 %back.1 = (f32[2304,1024]{1,0:T(8,128)}, f32[32,1024]{1,0:T(8,128)}, f32[64,1024]{1,0:T(8,128)}, f32[16,128]{1,0:T(8,128)}) custom-call(bf16[2304,2304]{1,0:T(8,128)(2,1)} %get-tuple-element.32.mix_ref, bf16[2304,1024]{1,0:T(8,128)(2,1)} %get-tuple-element.33.slope_ref, f32[128,1024]{1,0:T(8,128)} %copy-done.1, f32[8,1024]{1,0:T(8,128)} %copy-done.2, ...), custom_call_target="tpu_custom_call" | custom-call | tf_op jit(solution)/shard_map/back/pallas_call | solution.py:1163
  192.8 0.7 reshape.40
  193.5 0.1 constant_dynamic-slice_fusion
  193.6 0.5 slice_bitcast_fusion
  194.1 0.0 copy-start.6
  194.1 0.0 copy-start.5
  194.1 9.4 %copy.25 = f32[2304,1024]{1,0:T(8,128)} copy(f32[2304,1024]{1,0:T(8,128)} %get-tuple-element.53) | data formatting | bytes 18874368
  203.5 0.0 copy-done.6
  203.5 0.7 copy.26
  204.2 0.0 copy-done.5
  204.2 0.7 copy.27
Async XLA Ops:
  78.5 2.2 %copy-start = (bf16[2,2,2,2,2,64,1024]{6,5,4,3,2,1,0:T(8,128)(2,1)S(1)}, bf16[2,2,2,2,2,64,1024]{6,5,4,3,2,1,0:T(8,128)(2,1)}, u32[]{:S(2)}) copy-start(bf16[2,2,2,2,2,64,1024]{6,5,4,3,2,1,0:T(8,128)(2,1)} %get-tuple-element.29) | copy-start | bytes 12582916
  80.6 1.1 copy-start.3
  81.7 0.9 copy-start.4
  112.9 0.8 copy-start.1
  113.8 0.6 copy-start.2
  194.1 9.4 %copy-start.6 = (f32[32,1024]{1,0:T(8,128)S(1)}, f32[32,1024]{1,0:T(8,128)}, u32[]{:S(2)}) copy-start(f32[32,1024]{1,0:T(8,128)} %get-tuple-element.54) | copy-start | bytes 393220
  194.1 10.1 %copy-start.5 = (f32[64,1024]{1,0:T(8,128)S(1)}, f32[64,1024]{1,0:T(8,128)}, u32[]{:S(2)}) copy-start(f32[64,1024]{1,0:T(8,128)} %get-tuple-element.56) | copy-start | bytes 786436

commit v2 on v1

--- a/solution.py
+++ b/solution.py
@@ -13,11 +13,11 @@
 AXES = ("comm", "sub")
 
 
-def build_rows(index_ref, count_ref, importance_ref, own_ref, halo_ref, first, target, *, rows, halo):
+def build_rows(index_ref, count_ref, importance_ref, own_ref, halo_ref, first, *, rows, halo):
     his = (rows + halo + 255) // 256
     pairs = (his + 1) // 2
     fanout = index_ref.shape[0]
-    at = slice(first, first + 128)
+    at = pl.ds(pl.multiple_of(first, 128), 128)
     lane = lax.broadcasted_iota(jnp.int32, (16, 128), 1)
     sublane = lax.broadcasted_iota(jnp.int32, (16, 128), 0)
     parity = (sublane >= 8).astype(jnp.int32)
@@ -70,9 +70,9 @@
             )
         for h in range(his):
             tile = jnp.concatenate([t[h * 8 : (h + 1) * 8, :] for t in tiles], axis=0).astype(BF)
-            to = slice(first + g, first + g + 16)
+            to = pl.ds(pl.multiple_of(first + g, 16), 16)
             if h * 256 < rows:
-                own_ref[pl.ds(pl.multiple_of(target + g, 16), 16), h * 256 : (h + 1) * 256] = tile
+                own_ref[to, h * 256 : (h + 1) * 256] = tile
             else:
                 start = h * 256 - rows
                 stop = min(start + 256, halo)
@@ -81,7 +81,7 @@
 
 def build_kernel(index_ref, count_ref, importance_ref, own_ref, halo_ref, *, rows, halo):
     for first in range(0, own_ref.shape[0], 128):
-        build_rows(index_ref, count_ref, importance_ref, own_ref, halo_ref, first, first, rows=rows, halo=halo)
+        build_rows(index_ref, count_ref, importance_ref, own_ref, halo_ref, first, rows=rows, halo=halo)
 
 
 def build_mixing(nbr_index, nbr_count, importance, halo):
@@ -117,19 +117,21 @@
     return x * half, half + slope
 
 
-def hidden_rows(features_ref, q, bias, sent_rows, low_ref, neigh_ref, slope_ref, sent_ref, start):
-    block, width = features_ref.shape
-    at_rows = pl.ds(pl.multiple_of(start, block), block)
-    low_ref[...] = features_ref[...].astype(BF)
+def hidden_rows(features_ref, q_buf, bias_ref, send_ref, low_ref, neigh_ref, slope_ref, sent_ref, at_rows, start):
+    width = features_ref.shape[1]
+    lead = (slice(None),) * (len(q_buf.shape) - 1)
+    low_ref[at_rows, :] = features_ref[at_rows, :].astype(BF)
     for c in range(0, width, 256):
         at = slice(c, c + 256)
-        pre = jnp.dot(low_ref[...], q[:, at], preferred_element_type=F32) + bias[:, at]
+        q = q_buf[lead + (at,)].reshape(width, 256)
+        pre = jnp.dot(low_ref[at_rows, :], q, preferred_element_type=F32) + bias_ref[0:1, at]
         value, slope = gelu_pair(pre)
         neigh_ref[at_rows, at] = value.astype(BF)
-        slope_ref[:, at] = slope.astype(BF)
-    local = lax.broadcasted_iota(jnp.int32, (sent_rows.shape[0], block), 1) + start
-    chosen = jnp.where(local == sent_rows, 1.0, 0.0).astype(BF)
-    sent_ref[...] += jnp.dot(chosen, neigh_ref[at_rows, :], preferred_element_type=F32)
+        slope_ref[at_rows, at] = slope.astype(BF)
+    neigh = neigh_ref[at_rows, :]
+    local = lax.broadcasted_iota(jnp.int32, (send_ref.shape[0], neigh.shape[0]), 1) + start
+    chosen = jnp.where(local == send_ref[...], 1.0, 0.0).astype(BF)
+    sent_ref[...] += jnp.dot(chosen, neigh, preferred_element_type=F32)
 
 
 def ring_copies(groups, index, blocks_ref, landed_ref, send_sem, recv_sem, device_of):
@@ -175,22 +177,26 @@
     index_ref,
     count_ref,
     importance_ref,
-    features_ref,
     q_ref,
     w_ref,
     bias_ref,
     send_ref,
+    features_hbm,
     own_out,
     halo_ref,
-    low_ref,
-    slope_ref,
-    pooled_ref,
+    low_out,
+    slope_out,
+    pooled_out,
     incoming_ref,
     q_full,
     w_full,
     bias_out,
+    features,
     own_mix,
+    low,
     neigh,
+    slope,
+    pooled,
     q_buf,
     w_own,
     bias_buf,
@@ -200,7 +206,7 @@
     comm_blocks,
     comm_landed,
     local_sem,
-    mix_sem,
+    feature_sem,
     send_sem,
     recv_sem,
     sub_send,
@@ -214,13 +220,9 @@
     block,
     pool_block,
 ):
-    i = pl.program_id(0)
     rows = own_mix.shape[0]
     halo = halo_ref.shape[1]
     width = neigh.shape[1]
-    builds = rows // block
-    hidden_end = 2 * builds
-    steps = hidden_end + rows // pool_block
     comm, sub = lax.axis_index("comm"), lax.axis_index("sub")
     me = comm * subs + sub
     mine = [(me // (1 << b)) % 2 for b in range(bits)]
@@ -282,10 +284,6 @@
     q_local = pltpu.make_async_copy(q_buf, q_full, local_sem.at[1])
     last = len(chains["q"]) - 1
 
-    def mix_copy(step):
-        at = pl.ds(pl.multiple_of(step * block, block), block)
-        return pltpu.make_async_copy(own_mix.at[at, :], own_out.at[at, :], mix_sem)
-
     def begin(name, n):
         for c in chains[name][n]:
             c.start()
@@ -294,124 +292,118 @@
         for c in chains[name][n]:
             c.wait()
 
-    def happen(part):
-        for (step, at), names in events.items():
-            if at == part:
-
-                @pl.when(i == step)
+    def place(n, size):
+        return pl.ds(pl.multiple_of(n * size, size), size)
+
+    def feature_copy(n):
+        at = place(n, block)
+        return pltpu.make_async_copy(features_hbm.at[at, :], features.at[at, :], feature_sem.at[n])
+
+    outs = [(own_mix, own_out), (low, low_out), (slope, slope_out), (pooled, pooled_out)]
+
+    def give(n, at):
+        source, target = outs[n]
+        pltpu.make_async_copy(source.at[at, :], target.at[at, :], local_sem.at[2 + n]).start()
+
+    def given(n):
+        pltpu.make_async_copy(*outs[n], local_sem.at[2 + n]).wait()
+
+    events = {
+        ("build", 4): [("q", 0), ("bias", 0)],
+        ("build", 6): [("w0", -1)],
+        ("build", 7): [("q", 1), ("bias", 1)],
+        ("build", 9): [("w1", -1)],
+        ("build", 10): [("q", 2), ("bias", 2), ("w0", 0)],
+        ("build", 13): [("w1", 0)],
+        ("build", 14): [("w0", 1)],
+        ("build", 15): [("q", 3), ("bias", 3)],
+        ("hidden", 0): [("w1", 1)],
+        ("hidden", 1): [("w0", 2)],
+        ("hidden", 6): [("w0", 3), ("w1", 2)],
+        ("pool", 2): [("w1", 3)],
+    }
+
+    def happen(phase, n):
+        for (when, step), names in events.items():
+            if when == phase:
+
+                @pl.when(n == step)
                 def _(names=names):
-                    for name, n in names:
-                        if n >= 0:
-                            finish(name, n)
-                        if n < last:
-                            begin(name, n + 1)
-
-    @pl.when(i == 0)
-    def _():
-        q_buf[spot([])] = q_ref[...].astype(BF)
-        w_own[...] = w_ref[...].astype(BF)
-        bias_buf[spot([])] = bias_ref[...]
-        sent_acc[...] = jnp.zeros_like(sent_acc)
-        w_local.start()
-        greet(comm, sub, comms, subs)
-        begin("q", 0)
-        begin("bias", 0)
-        w_local.wait()
-
-    events = {
-        (0, 1): [("w0", -1)],
-        (2, 0): [("q", 0), ("bias", 0)],
-        (3, 0): [("w0", 0), ("w1", -1)],
-        (3, 1): [("q", 1), ("bias", 1)],
-        (4, 1): [("w0", 1)],
-        (5, 0): [("q", 2), ("bias", 2)],
-        (5, 1): [("w1", 0)],
-        (7, 0): [("w0", 2), ("w1", 1)],
-        (8, 0): [("q", 3), ("bias", 3)],
-        (builds + 2, 0): [("w0", 3)],
-        (builds + 4, 0): [("w1", 2)],
-        (hidden_end, 0): [("w0", 4)],
-        (hidden_end + 1, 0): [("w1", 3)],
-    }
-
-    happen(0)
-    for part in range(block // 128):
-        if part == 1:
-            happen(1)
-
-        @pl.when(i < builds)
-        def _(part=part):
-            build_rows(
-                index_ref,
-                count_ref,
-                importance_ref,
-                own_mix,
-                halo_ref,
-                part * 128,
-                i * block + part * 128,
-                rows=rows,
-                halo=halo,
-            )
-
-    @pl.when(i < builds)
-    def _():
-        mix_copy(i).start()
-
-    @pl.when(i == builds)
-    def _():
-        finish("q", last)
-        finish("bias", last)
-        q_local.start()
-        share = width >> bits
-        for k in range(2):
-            pieces = []
-            for e in range(1 << bits):
-                piece = bias_buf[tuple((e >> b) & 1 for b in order)]
-                pieces.append(piece[0:1, k * share : (k + 1) * share])
-            bias_out[k : k + 1, :] = jnp.concatenate(pieces, axis=1).astype(BF).astype(F32)
-        bias_out[2:, :] = jnp.zeros((6, width), F32)
-
-    @pl.when(jnp.logical_and(i >= builds, i < hidden_end))
-    def _():
-        mix_copy(i - builds).wait()
-        q = q_buf[...].reshape(width, width)
-        hidden_rows(
-            features_ref,
-            q,
-            bias_out[0:1, :],
-            send_ref[...],
-            low_ref,
-            neigh,
-            slope_ref,
-            sent_acc,
-            (i - builds) * block,
+                    for name, k in names:
+                        if k >= 0:
+                            finish(name, k)
+                        begin(name, k + 1)
+
+    q_buf[spot([])] = q_ref[...].astype(BF)
+    w_own[...] = w_ref[...].astype(BF)
+    bias_buf[spot([])] = bias_ref[...]
+    greet(comm, sub, comms, subs)
+    begin("q", 0)
+    begin("bias", 0)
+    w_local.start()
+    sent_acc[...] = jnp.zeros_like(sent_acc)
+    w_local.wait()
+
+    @pl.loop(0, rows // block)
+    def _(n):
+        feature_copy(n).start()
+
+    @pl.loop(0, rows // 128)
+    def _(n):
+        happen("build", n)
+        build_rows(
+            index_ref, count_ref, importance_ref, own_mix, halo_ref, n * 128, rows=rows, halo=halo
         )
-
-    @pl.when(i == hidden_end - 1)
-    def _():
-        sub_blocks[...] = sent_acc[...].astype(BF).reshape(sub_blocks.shape)
-        begin("sub", 0)
-        sub_landed[sub] = sub_blocks[sub]
-
-    @pl.when(i == hidden_end + 2)
-    def _():
-        finish("sub", 0)
-        moved = regroup(sub_landed[...].reshape(halo, width), subs, comms, halo // (subs * comms))
-        comm_blocks[...] = moved.reshape(comm_blocks.shape)
-        begin("comm", 0)
-        comm_landed[comm] = comm_blocks[comm]
-
-    @pl.when(i >= hidden_end)
-    def _():
-        at = pl.ds(pl.multiple_of((i - hidden_end) * pool_block, pool_block), pool_block)
-        pooled_ref[...] = jnp.dot(own_mix[at, :], neigh[...], preferred_element_type=F32)
-
-    @pl.when(i == steps - 1)
-    def _():
-        finish("w1", last)
-        q_local.wait()
-        finish("comm", 0)
-        incoming_ref[...] = comm_landed[...].reshape(halo, width)
+        give(0, place(n, 128))
+
+    finish("q", last)
+    finish("bias", last)
+    q_local.start()
+    share = width >> bits
+    for k in range(2):
+        pieces = []
+        for e in range(1 << bits):
+            piece = bias_buf[tuple((e >> b) & 1 for b in order)]
+            pieces.append(piece[0:1, k * share : (k + 1) * share])
+        bias_out[k : k + 1, :] = jnp.concatenate(pieces, axis=1).astype(BF).astype(F32)
+    bias_out[2:, :] = jnp.zeros((6, width), F32)
+
+    @pl.loop(0, rows // block)
+    def _(n):
+        happen("hidden", n)
+        feature_copy(n).wait()
+        at = place(n, block)
+        hidden_rows(features, q_buf, bias_out, send_ref, low, neigh, slope, sent_acc, at, n * block)
+        give(1, at)
+        give(2, at)
+
+    sub_blocks[...] = sent_acc[...].astype(BF).reshape(sub_blocks.shape)
+    begin("sub", 0)
+    sub_landed[sub] = sub_blocks[sub]
+
+    @pl.loop(0, rows // pool_block)
+    def _(n):
+        happen("pool", n)
+
+        @pl.when(n == 2)
+        def _():
+            finish("sub", 0)
+            moved = regroup(sub_landed[...].reshape(halo, width), subs, comms, halo // (subs * comms))
+            comm_blocks[...] = moved.reshape(comm_blocks.shape)
+            begin("comm", 0)
+            comm_landed[comm] = comm_blocks[comm]
+
+        at = place(n, pool_block)
+        pooled[at, :] = jnp.dot(own_mix[at, :], neigh[...], preferred_element_type=F32)
+        give(3, at)
+
+    finish("w0", last)
+    finish("w1", last)
+    finish("comm", 0)
+    incoming_ref[...] = comm_landed[...].reshape(halo, width)
+    q_local.wait()
+    for n in range(4):
+        given(n)
 
 
 def gather_and_transform(features, q_weight, q_bias, w_weight, w_bias, nbr_index, nbr_count, importance, send_rows):
@@ -423,55 +415,21 @@
     per = send_rows.shape[2]
     halo = devices * per
     block, pool_block = 256, 384
-    builds = rows // block
     q_rows, w_rows = q_weight.shape[0], w_weight.shape[0]
     share = q_bias.shape[0]
     bias_tile = jnp.pad(jnp.concatenate([q_bias, w_bias])[None], ((0, 7), (0, 128 - 2 * share)))
     by_sub = send_rows.reshape(comms, subs, per).transpose(1, 0, 2).reshape(halo, 1)
     lead = (2,) * bits
 
-    def built(i):
-        return (jnp.minimum(i, builds - 1), 0)
-
-    def built_columns(i):
-        return (0, jnp.minimum(i, builds - 1))
-
-    def later(i):
-        return (jnp.clip(i - builds, 0, builds - 1), 0)
-
-    def pooled_at(i):
-        return (jnp.maximum(i - 2 * builds, 0), 0)
-
-    def whole(*shape):
-        return pl.BlockSpec(shape, lambda i: (0,) * len(shape))
-
+    here = pl.BlockSpec(memory_space=pltpu.VMEM)
+    anywhere = pl.BlockSpec(memory_space=pl.ANY)
     copies = 4 * bits + 3 * 2
     out = pl.pallas_call(
         functools.partial(
             gather_kernel, comms=comms, subs=subs, bits=bits, block=block, pool_block=pool_block
         ),
-        grid=(2 * builds + rows // pool_block,),
-        in_specs=[
-            pl.BlockSpec((fanout, block), built_columns),
-            pl.BlockSpec((1, block), built_columns),
-            pl.BlockSpec((fanout, block), built_columns),
-            pl.BlockSpec((block, width), later),
-            whole(q_rows, width),
-            whole(w_rows, width),
-            whole(8, 128),
-            whole(halo, 1),
-        ],
-        out_specs=[
-            pl.BlockSpec(memory_space=pl.ANY),
-            pl.BlockSpec((block, halo), built),
-            pl.BlockSpec((block, width), later),
-            pl.BlockSpec((block, width), later),
-            pl.BlockSpec((pool_block, width), pooled_at),
-            whole(halo, width),
-            pl.BlockSpec(memory_space=pl.ANY),
-            pl.BlockSpec(memory_space=pl.ANY),
-            whole(8, width),
-        ],
+        in_specs=[here] * 7 + [anywhere],
+        out_specs=[anywhere, here, anywhere, anywhere, anywhere, here, anywhere, anywhere, here],
         out_shape=[
             jax.ShapeDtypeStruct((rows, rows), BF),
             jax.ShapeDtypeStruct((rows, halo), BF),
@@ -484,8 +442,12 @@
             jax.ShapeDtypeStruct((8, width), F32),
         ],
         scratch_shapes=[
+            pltpu.VMEM((rows, width), F32),
             pltpu.VMEM((rows, rows), BF),
             pltpu.VMEM((rows, width), BF),
+            pltpu.VMEM((rows, width), BF),
+            pltpu.VMEM((rows, width), BF),
+            pltpu.VMEM((rows, width), F32),
             pltpu.VMEM(lead + (q_rows, width), BF),
             pltpu.VMEM((w_rows, width), BF),
             pltpu.VMEM(lead + (8, 128), F32),
@@ -494,8 +456,8 @@
             pltpu.VMEM((subs, halo // subs, width), BF),
             pltpu.VMEM((comms, halo // comms, width), BF),
             pltpu.VMEM((comms, halo // comms, width), BF),
-            pltpu.SemaphoreType.DMA((2,)),
-            pltpu.SemaphoreType.DMA,
+            pltpu.SemaphoreType.DMA((6,)),
+            pltpu.SemaphoreType.DMA((rows // block,)),
             pltpu.SemaphoreType.DMA((copies,)),
             pltpu.SemaphoreType.DMA((copies,)),
             pltpu.SemaphoreType.DMA((subs - 1,)),
@@ -504,18 +466,18 @@
             pltpu.SemaphoreType.DMA((comms - 1,)),
         ],
         compiler_params=pltpu.CompilerParams(
-            collective_id=0, has_side_effects=True, vmem_limit_bytes=56 * 2**20
+            collective_id=0, has_side_effects=True, vmem_limit_bytes=62 * 2**20
         ),
         name="gather_and_transform",
     )(
         nbr_index.T,
         nbr_count.reshape(1, rows),
         importance.T,
-        features,
         q_weight,
         w_weight,
         bias_tile,
         by_sub,
+        features,
     )
     own_mix, halo_mix, low, slope, pooled_own, incoming, q_full, w_full, biases = out
     return (
@@ -678,7 +640,7 @@
             jax.ShapeDtypeStruct((8, width), F32),
         ],
         scratch_shapes=[pltpu.VMEM((block, width), F32), pltpu.VMEM((block, width), F32)],
-        compiler_params=pltpu.CompilerParams(vmem_limit_bytes=48 * 2**20),
+        compiler_params=pltpu.CompilerParams(vmem_limit_bytes=62 * 2**20),
         cost_estimate=pl.CostEstimate(
             flops=6 * rows * width * width, bytes_accessed=22 * rows * width, transcendentals=rows * width
         ),
@@ -854,26 +816,29 @@
 
 
 def back_body(
-    mix_ref,
-    slope_ref,
     sent_grad_ref,
     w_bias_ref,
     target_ref,
+    mix_hbm,
+    slope_hbm,
     low_hbm,
     pooled_hbm,
     out_hbm,
     grad_pooled_hbm,
     w_hbm,
     q_hbm,
-    features_ref,
+    features_out,
     q_out,
     w_out,
     bias_out,
     joined,
     grad_out,
     grad_pooled,
+    slope,
     w_top,
     q_full,
+    mix,
+    features,
     q_bias_acc,
     bias_sent,
     bias_got,
@@ -889,8 +854,7 @@
     row_block,
 ):
     sets = [rest[7 * k : 7 * k + 7] for k in range(3)]
-    load_sem, bias_send, bias_recv, comm_send, comm_recv, sub_send, sub_recv = rest[21:]
-    i = pl.program_id(0)
+    load_sem, mix_sem, out_sem, bias_send, bias_recv, comm_send, comm_recv, sub_send, sub_recv = rest[21:]
     rows, width = grad_out.shape
     halo = sent_grad_ref.shape[0]
     half = width // 2
@@ -918,6 +882,7 @@
         (pooled_hbm.at[:, right], joined.at[:, pl.ds(3 * half, half)]),
         (out_hbm.at[:, right], grad_out.at[:, right]),
         (grad_pooled_hbm, grad_pooled),
+        (slope_hbm, slope),
         (w_hbm.at[pl.ds(0, width), :], w_top),
         (q_hbm, q_full),
     ]
@@ -936,46 +901,16 @@
         for b in range(bits)
     ]
 
-    products = 8
     spreads = rows // mix_block
-    spread_end = products + spreads
-    q_end = spread_end + 4
-    steps = q_end + rows // row_block
-
-    def load_wait(step, which):
-        @pl.when(i == step)
-        def _():
-            for n in which:
-                loads[n].wait()
-
-    @pl.when(i == 0)
-    def _():
-        for c in loads:
-            c.start()
-        greet(comm, sub, comms, subs)
-        comm_blocks[...] = sent_grad_ref[...].astype(BF).reshape(comm_blocks.shape)
-        for c in comm_ring:
-            c.start()
-        comm_landed[comm] = comm_blocks[comm]
-        q_bias_acc[...] = jnp.zeros_like(q_bias_acc)
-
-    load_wait(0, [0, 1])
-    load_wait(1, [2])
-    load_wait(2, [3])
-    load_wait(3, [4])
-    load_wait(4, [5])
-    load_wait(products, [6])
-    load_wait(q_end, [7, 8])
-
-    @pl.when(i == 2)
-    def _():
-        for c in comm_ring:
-            c.wait()
-        moved = regroup(comm_landed[...].reshape(halo, width), comms, subs, halo // (subs * comms))
-        sub_blocks[...] = moved.reshape(sub_blocks.shape)
-        for c in sub_ring:
-            c.start()
-        sub_landed[sub] = sub_blocks[sub]
+    rounds = rows // row_block
+
+    def mix_copy(n):
+        at = pl.ds(pl.multiple_of(n * mix_block, mix_block), mix_block)
+        return pltpu.make_async_copy(mix_hbm.at[:, at], mix.at[n % 2], mix_sem.at[n % 2])
+
+    def out_copy(n):
+        at = pl.ds(pl.multiple_of(n * row_block, row_block), row_block)
+        return pltpu.make_async_copy(features.at[n % 2], features_out.at[at, :], out_sem.at[n % 2])
 
     def step_of(which, k):
         which.wait(k)
@@ -996,79 +931,101 @@
     def w_top_bits(j):
         return ((j // 2) % 2, j % 2)
 
+    events = {
+        ("w1", 1): [(0, 0)],
+        ("spread", 1): [(1, 0), (0, 1)],
+        ("spread", 3): [(0, 2)],
+        ("spread", 4): [(1, 1)],
+        ("spread", 5): [(0, 3)],
+        ("q", 1): [(1, 2), (0, 4)],
+        ("q", 3): [(1, 3)],
+        ("features", 1): [(1, 4), (2, 0)],
+        ("features", 4): [(2, 1)],
+    }
+    all_sets = w_sets + [q_set]
+
+    def happen(phase, n):
+        for (when, step), which in events.items():
+            if when == phase:
+
+                @pl.when(n == step)
+                def _(which=which):
+                    for m, k in which:
+                        step_of(all_sets[m], k)
+
+    def load_when(step, n, begin=(), need=()):
+        @pl.when(n == step)
+        def _():
+            for m in need:
+                loads[m].wait()
+            for m in begin:
+                loads[m].start()
+
+    for n in range(3):
+        loads[n].start()
+    comm_blocks[...] = sent_grad_ref[...].astype(BF).reshape(comm_blocks.shape)
+    q_bias_acc[...] = jnp.zeros_like(q_bias_acc)
+    greet(comm, sub, comms, subs)
+    for c in comm_ring:
+        c.start()
+    comm_landed[comm] = comm_blocks[comm]
+
     for n in range(2):
 
-        @pl.when(jnp.logical_and(i >= 4 * n, i < 4 * n + 4))
-        def _(n=n):
-            j = i - 4 * n
+        @pl.loop(0, 4)
+        def _(j, n=n):
+            if n == 0:
+                load_when(0, j, [3], [0, 1])
+                load_when(1, j, [4], [2])
+                load_when(2, j, [5], [3])
+                load_when(3, j, [6], [4])
+            else:
+                load_when(0, j, [7], [5])
+                load_when(1, j, [8])
+                load_when(2, j, [9])
+
+                @pl.when(j == 3)
+                def _():
+                    mix_copy(0).start()
+
             at = pl.ds(pl.multiple_of(j * half, half), half)
             columns = slice(n * half, (n + 1) * half)
             value = lax.dot_general(joined[:, at], grad_out[:, columns], tn, preferred_element_type=F32)
             deal(value, w_sets[n], w_top_bits(j), w_out.shape[0])
-            for t in range(4):
-
-                @pl.when(j == t)
-                def _(t=t):
-                    w_sets[n].first(t).start()
-
-    events = {
-        5: [(0, 0)],
-        products + 1: [(1, 0), (0, 1)],
-        products + 3: [(0, 2)],
-        products + 4: [(1, 1)],
-        products + 5: [(0, 3)],
-        spread_end + 1: [(1, 2), (0, 4)],
-        spread_end + 3: [(1, 3)],
-        q_end + 1: [(1, 4)],
-    }
-    for step, which in events.items():
-
-        @pl.when(i == step)
-        def _(which=which):
-            for n, k in which:
-                step_of(w_sets[n], k)
-
-    @pl.when(i == products)
-    def _():
-        for c in sub_ring:
-            c.wait()
-
-    @pl.when(jnp.logical_and(i >= products, i < spread_end))
-    def _():
-        start = (i - products) * mix_block
+            w_sets[n].first(j).start()
+            happen("w" + str(n), j)
+
+        if n == 0:
+            for c in comm_ring:
+                c.wait()
+            moved = regroup(comm_landed[...].reshape(halo, width), comms, subs, halo // (subs * comms))
+            sub_blocks[...] = moved.reshape(sub_blocks.shape)
+            for c in sub_ring:
+                c.start()
+            sub_landed[sub] = sub_blocks[sub]
+
+    for c in sub_ring:
+        c.wait()
+    for n in (6, 7):
+        loads[n].wait()
+
+    @pl.loop(0, spreads)
+    def _(n):
+        @pl.when(n + 1 < spreads)
+        def _():
+            mix_copy(n + 1).start()
+
+        happen("spread", n)
+        mix_copy(n).wait()
+        start = n * mix_block
+        at = pl.ds(pl.multiple_of(start, mix_block), mix_block)
         local = lax.broadcasted_iota(jnp.int32, (mix_block, halo), 0) + start
         chosen = jnp.where(local == target_ref[...], 1.0, 0.0).astype(BF)
-        back = lax.dot_general(mix_ref[...], grad_pooled[...], tn, preferred_element_type=F32)
+        back = lax.dot_general(mix[n % 2], grad_pooled[...], tn, preferred_element_type=F32)
         back += jnp.dot(chosen, sub_landed[...].reshape(halo, width), preferred_element_type=F32)
-        grad = (back * slope_ref[...].astype(F32)).astype(BF)
-        joined[pl.ds(pl.multiple_of(start, 128), mix_block), width:] = grad
+        grad = (back * slope[at, :].astype(F32)).astype(BF)
+        joined[at, width:] = grad
         q_bias_acc[0:1, :] += jnp.sum(grad.astype(F32), axis=0, keepdims=True)
-
-    @pl.when(jnp.logical_and(i >= spread_end, i < q_end))
-    def _():
-        for t in range(4):
-
-            @pl.when(i == spread_end + t)
-            def _(t=t):
-                n, j = t % 2, t // 2
-                value = lax.dot_general(
-                    joined[:, j * half : (j + 1) * half],
-                    joined[:, width + n * half : width + (n + 1) * half],
-                    tn,
-                    preferred_element_type=F32,
-                )
-                keep_even = mine[0] == 0
-                columns = slice(n * half, (n + 1) * half)
-                each = q_out.shape[0]
-                for p in range(half // each // 2):
-                    even = value[2 * p * each : (2 * p + 1) * each]
-                    odd = value[(2 * p + 1) * each : (2 * p + 2) * each]
-                    at = (j, (p >> 2) & 1, (p >> 1) & 1, p & 1, slice(None), columns)
-                    q_set.held[at] = jnp.where(keep_even, even, odd)
-                    q_set.sent[at] = jnp.where(keep_even, odd, even).astype(BF)
-                if n == 1:
-                    q_set.first(2 * j).start()
-                    q_set.first(2 * j + 1).start()
 
     def bias_step(b):
         if b:
@@ -1080,41 +1037,60 @@
             bias_sent[b] = total
         bias_copies[b].start()
 
-    @pl.when(i == spread_end)
-    def _():
-        pieces = [w_bias_ref[0:1, c : c + 128] for c in range(0, width, 128)]
-        pieces += [q_bias_acc[0:1, c : c + 128] for c in range(0, width, 128)]
-        bias_sent[0] = jnp.concatenate(pieces, axis=0)
-
-    for b in range(bits):
-
-        @pl.when(i == spread_end + b)
-        def _(b=b):
-            bias_step(b)
-
-    q_events = {q_end + 1: 0, q_end + 4: 1}
-    for step, k in q_events.items():
-
-        @pl.when(i == step)
-        def _(k=k):
-            step_of(q_set, k)
-
-    @pl.when(i >= q_end)
-    def _():
-        at = pl.ds(pl.multiple_of((i - q_end) * row_block, 128), row_block)
+    pieces = [w_bias_ref[0:1, c : c + 128] for c in range(0, width, 128)]
+    pieces += [q_bias_acc[0:1, c : c + 128] for c in range(0, width, 128)]
+    bias_sent[0] = jnp.concatenate(pieces, axis=0)
+
+    for t in range(4):
+        bias_step(t)
+        n, j = t % 2, t // 2
+        value = lax.dot_general(
+            joined[:, j * half : (j + 1) * half],
+            joined[:, width + n * half : width + (n + 1) * half],
+            tn,
+            preferred_element_type=F32,
+        )
+        keep_even = mine[0] == 0
+        columns = slice(n * half, (n + 1) * half)
+        each = q_out.shape[0]
+        for p in range(half // each // 2):
+            even = value[2 * p * each : (2 * p + 1) * each]
+            odd = value[(2 * p + 1) * each : (2 * p + 2) * each]
+            at = (j, (p >> 2) & 1, (p >> 1) & 1, p & 1, slice(None), columns)
+            q_set.held[at] = jnp.where(keep_even, even, odd)
+            q_set.sent[at] = jnp.where(keep_even, odd, even).astype(BF)
+        if n == 1:
+            q_set.first(2 * j).start()
+            q_set.first(2 * j + 1).start()
+        for m, k in events.get(("q", t), []):
+            step_of(all_sets[m], k)
+    bias_step(4)
+    for n in (8, 9):
+        loads[n].wait()
+
+    @pl.loop(0, rounds)
+    def _(n):
+        happen("features", n)
+
+        @pl.when(n >= 2)
+        def _():
+            out_copy(n - 2).wait()
+
+        at = pl.ds(pl.multiple_of(n * row_block, row_block), row_block)
         value = lax.dot_general(grad_out[at, :], w_top[...], nt, preferred_element_type=F32)
-        features_ref[...] = value + lax.dot_general(
+        features[n % 2] = value + lax.dot_general(
             joined[at, width:], q_full[...], nt, preferred_element_type=F32
         )
-
-    @pl.when(i == steps - 1)
-    def _():
-        for k in range(2, bits):
-            step_of(q_set, k)
-        for n in range(2):
-            w_out[:, n * half : (n + 1) * half] = w_sets[n].result()
-        q_out[...] = q_set.result()
-        bias_step(bits)
+        out_copy(n).start()
+
+    for k in range(2, bits):
+        step_of(q_set, k)
+    for n in range(2):
+        w_out[:, n * half : (n + 1) * half] = w_sets[n].result()
+    q_out[...] = q_set.result()
+    bias_step(bits)
+    for n in range(rounds - 2, rounds):
+        out_copy(n).wait()
 
 
 def back_kernel(
@@ -1127,9 +1103,6 @@
     per = send_rows.shape[2]
     halo = devices * per
     mix_block, row_block = 384, 384
-    spreads = rows // mix_block
-    spread_end = 8 + spreads
-    q_end = spread_end + 4
     w_rows, q_rows = w_full.shape[0] // devices, q_full.shape[0] // devices
     targets = send_rows.reshape(comms, subs, per).transpose(1, 0, 2).reshape(1, halo)
     lead = (2,) * (bits - 1)
@@ -1147,38 +1120,14 @@
             pltpu.SemaphoreType.DMA((copies,)),
         ]
 
-    def spread_columns(i):
-        return (0, jnp.clip(i - 8, 0, spreads - 1))
-
-    def spread_rows(i):
-        return (jnp.clip(i - 8, 0, spreads - 1), 0)
-
-    def whole(*shape):
-        return pl.BlockSpec(shape, lambda i: (0,) * len(shape), pipeline_mode=pl.Buffered(1))
-
-    def whole_out(*shape):
-        return pl.BlockSpec(shape, lambda i: (0,) * len(shape))
-
+    here = pl.BlockSpec(memory_space=pltpu.VMEM)
     anywhere = pl.BlockSpec(memory_space=pl.ANY)
     grad_features, grad_q, grad_w, biases = pl.pallas_call(
         functools.partial(
             back_body, comms=comms, subs=subs, bits=bits, mix_block=mix_block, row_block=row_block
         ),
-        grid=(q_end + rows // row_block,),
-        in_specs=[
-            pl.BlockSpec((rows, mix_block), spread_columns),
-            pl.BlockSpec((mix_block, width), spread_rows),
-            whole(halo, width),
-            whole(8, width),
-            whole(1, halo),
-        ]
-        + [anywhere] * 6,
-        out_specs=[
-            pl.BlockSpec((row_block, width), lambda i: (jnp.maximum(i - q_end, 0), 0)),
-            whole_out(q_rows, width),
-            whole_out(w_rows, width),
-            whole_out(16, 128),
-        ],
+        in_specs=[here] * 3 + [anywhere] * 8,
+        out_specs=[anywhere] + [here] * 3,
         out_shape=[
             jax.ShapeDtypeStruct((rows, width), F32),
             jax.ShapeDtypeStruct((q_rows, width), F32),
@@ -1189,8 +1138,11 @@
             pltpu.VMEM((rows, 2 * width), BF),
             pltpu.VMEM((rows, width), BF),
             pltpu.VMEM((rows, width), BF),
+            pltpu.VMEM((rows, width), BF),
             pltpu.VMEM((width, width), BF),
             pltpu.VMEM((width, width), BF),
+            pltpu.VMEM((2, rows, mix_block), BF),
+            pltpu.VMEM((2, row_block, width), F32),
             pltpu.VMEM((8, width), F32),
             pltpu.VMEM((bits, 16, 128), F32),
             pltpu.VMEM((bits, 16, 128), F32),
@@ -1203,7 +1155,9 @@
         + set_scratch(w_rows, width // 2)
         + set_scratch(q_rows, width)
         + [
-            pltpu.SemaphoreType.DMA((9,)),
+            pltpu.SemaphoreType.DMA((10,)),
+            pltpu.SemaphoreType.DMA((2,)),
+            pltpu.SemaphoreType.DMA((2,)),
             pltpu.SemaphoreType.DMA((bits,)),
             pltpu.SemaphoreType.DMA((bits,)),
             pltpu.SemaphoreType.DMA((comms - 1,)),
@@ -1215,7 +1169,7 @@
             collective_id=1, has_side_effects=True, vmem_limit_bytes=62 * 2**20
         ),
         name="back",
-    )(own_mix, slope, sent_grad, grad_wbias, targets, low, pooled, grad_out, grad_pooled, w_full, q_full)
+    )(sent_grad, grad_wbias, targets, own_mix, slope, low, pooled, grad_out, grad_pooled, w_full, q_full)
     share = width // devices
     sums = lax.dynamic_slice_in_dim(biases.reshape(2, width), lax.axis_index(AXES) * share, share, 1)
     return grad_features, grad_q, sums[1], grad_w, sums[0]

time: 205 us -> 183 us (0.89)
  Pallas kernels: 181 us -> 164 us
  local copies, waits for them, and re-layouts: 22.6 us -> 17.6 us
    pallas_call x1, Pallas kernels: 72.2 us -> 62.7 us  [gather_and_transform(): pl.pallas_call(functools.partial(gather_kernel, comms=comms, subs=subs, b...]
    pallas_call x1, Pallas kernels: 78.4 us -> 69.8 us  [back_kernel(): pl.pallas_call(functools.partial(back_body, comms=comms, subs=subs, bits=...]
    unnamed x17 -> x7, local copies, waits for them, and re-layouts: 16.4 us -> 10.8 us
where the time goes in v2:
time: 183 us
  Pallas kernels  164 us (90%)
  local copies, waits for them, and re-layouts  17.6 us (10%)
    pallas_call x1, Pallas kernels, back_kernel(): pl.pallas_call(functools.partial(back_body, comms=comms, subs=subs, bits=...  69.8 us
    pallas_call x1, Pallas kernels, gather_and_transform(): pl.pallas_call(functools.partial(gather_kernel, comms=comms, subs=subs, b...  62.7 us
    pallas_call x1, Pallas kernels, combine(): pl.pallas_call(combine_kernel, grid=(rows // block,), in_specs=[by_rows(b...  31.2 us
    unnamed x7, local copies, waits for them, and re-layouts  10.8 us

profile of v2, /device:TPU:0, one launch (start us, length us, event | category | flops | bytes accessed | tf_op | source)
XLA Modules:
  0.0 182.7 jit_solution(17005308726733350510)
XLA Ops:
  0.6 0.7 maximum_bitcast_fusion
  1.4 0.6 pad.4.bias_ref
  2.0 1.3 reshape.34.count_ref
  3.3 0.8 reshape.35
  4.1 0.1 copy.19
  4.2 0.6 reshape.38.target_ref
  4.8 0.7 reshape.41.send_ref
  5.5 62.7 %gather_and_transform.1 = (bf16[2304,2304]{1,0:T(8,128)(2,1)}, bf16[2304,128]{1,0:T(8,128)(2,1)}, bf16[2304,1024]{1,0:T(8,128)(2,1)}, bf16[2304,1024]{1,0:T(8,12...) custom-call(s32[50,2304]{1,0:T(8,128)} %bitcast.16, ...), custom_call_target="tpu_custom_call" | custom-call | tf_op jit(solution)/shard_map/gather_and_transform/pallas_call | solution.py:427
  68.3 1.4 slice.9.bias_ref
  69.6 31.2 %combine.1 = (f32[2304,1024]{1,0:T(8,128)}, bf16[2304,1024]{1,0:T(8,128)(2,1)}, bf16[2304,1024]{1,0:T(8,128)(2,1)}, bf16[2304,1024]{1,0:T(8,128)(2,1)}, f32[128,1024]{1,0:T(8,128)}, /*index=5*/f32[8,1024]{1,0:T(8,128)}) custom-call(f32[2304,1024]{1,0:T(8,128)} %get-tuple-element.25.own_ref, bf16[2304,128]{1,0:T(8,128)(2,1)} %get-tuple-element.26.halo_ref, ...), custom_call_target="tpu_custom_call" | custom-call | flops 14495514624 | bytes 51904512 | tf_op jit(solution)/shard_map/combine/pallas_call | solution.py:614
  100.8 69.8 %back.1 = (f32[2304,1024]{1,0:T(8,128)}, f32[32,1024]{1,0:T(8,128)}, f32[64,1024]{1,0:T(8,128)}, f32[16,128]{1,0:T(8,128)}) custom-call(f32[128,1024]{1,0:T(8,128)} %get-tuple-element.32.sent_grad_ref, f32[8,1024]{1,0:T(8,128)} %get-tuple-element.33.w_bias_ref, s32[1,128]{1,0:T(1,128)} %reshape.38.target_ref, bf16[2304,2304]{1,0:T(8,128)(2,1)} %get-tuple-element.34.mix_hbm, ...), custom_call_target="tpu_custom_call" | custom-call | tf_op jit(solution)/shard_map/back/pallas_call | solution.py:1125
  170.6 0.7 reshape.40
  171.3 0.1 constant_dynamic-slice_fusion
  171.4 0.5 slice_bitcast_fusion
  171.9 0.0 copy-start.1
  171.9 0.0 copy-start
  171.9 9.4 %copy.25 = f32[2304,1024]{1,0:T(8,128)} copy(f32[2304,1024]{1,0:T(8,128)} %get-tuple-element.53) | data formatting | bytes 18874368
  181.3 0.0 copy-done.1
  181.3 0.7 copy.26
  182.0 0.0 copy-done
  182.0 0.7 copy.27
Async XLA Ops:
  171.9 9.4 %copy-start.1 = (f32[32,1024]{1,0:T(8,128)S(1)}, f32[32,1024]{1,0:T(8,128)}, u32[]{:S(2)}) copy-start(f32[32,1024]{1,0:T(8,128)} %get-tuple-element.54) | copy-start | bytes 393220
  171.9 10.1 %copy-start = (f32[64,1024]{1,0:T(8,128)S(1)}, f32[64,1024]{1,0:T(8,128)}, u32[]{:S(2)}) copy-start(f32[64,1024]{1,0:T(8,128)} %get-tuple-element.56) | copy-start | bytes 786436

commit v3 on v2

--- a/solution.py
+++ b/solution.py
@@ -13,7 +13,7 @@
 AXES = ("comm", "sub")
 
 
-def build_rows(index_ref, count_ref, importance_ref, own_ref, halo_ref, first, *, rows, halo):
+def build_rows(index_ref, counts, importance_ref, own_ref, halo_ref, first, *, rows, halo):
     his = (rows + halo + 255) // 256
     pairs = (his + 1) // 2
     fanout = index_ref.shape[0]
@@ -38,7 +38,7 @@
 
     index = index_ref[:, at]
     slot = lax.broadcasted_iota(jnp.int32, index.shape, 0)
-    weight = jnp.where(slot < count_ref[:, at], importance_ref[:, at], 0.0)
+    weight = jnp.where(slot < counts, importance_ref[:, at], 0.0)
     alpha = by_row(weight / jnp.sum(weight, axis=0, keepdims=True))
     hi = by_row((index >> 8).astype(F32))
     lo = slots((index & 255).astype(F32)).astype(BF)
@@ -81,7 +81,8 @@
 
 def build_kernel(index_ref, count_ref, importance_ref, own_ref, halo_ref, *, rows, halo):
     for first in range(0, own_ref.shape[0], 128):
-        build_rows(index_ref, count_ref, importance_ref, own_ref, halo_ref, first, rows=rows, halo=halo)
+        counts = count_ref[:, first : first + 128]
+        build_rows(index_ref, counts, importance_ref, own_ref, halo_ref, first, rows=rows, halo=halo)
 
 
 def build_mixing(nbr_index, nbr_count, importance, halo):
@@ -129,9 +130,9 @@
         neigh_ref[at_rows, at] = value.astype(BF)
         slope_ref[at_rows, at] = slope.astype(BF)
     neigh = neigh_ref[at_rows, :]
-    local = lax.broadcasted_iota(jnp.int32, (send_ref.shape[0], neigh.shape[0]), 1) + start
+    local = lax.broadcasted_iota(jnp.int32, (neigh.shape[0], send_ref.shape[1]), 0) + start
     chosen = jnp.where(local == send_ref[...], 1.0, 0.0).astype(BF)
-    sent_ref[...] += jnp.dot(chosen, neigh, preferred_element_type=F32)
+    sent_ref[...] += lax.dot_general(chosen, neigh, (((0,), (0,)), ((), ())), preferred_element_type=F32)
 
 
 def ring_copies(groups, index, blocks_ref, landed_ref, send_sem, recv_sem, device_of):
@@ -173,13 +174,19 @@
     pl.semaphore_wait(barrier, comms + subs - 2)
 
 
+def send_targets(send_rows, comms, subs):
+    per = send_rows.shape[2]
+    return send_rows.reshape(comms, subs, per).transpose(1, 0, 2).reshape(1, comms * subs * per)
+
+
 def gather_kernel(
     index_ref,
     count_ref,
     importance_ref,
     q_ref,
     w_ref,
-    bias_ref,
+    q_bias_ref,
+    w_bias_ref,
     send_ref,
     features_hbm,
     own_out,
@@ -336,7 +343,11 @@
 
     q_buf[spot([])] = q_ref[...].astype(BF)
     w_own[...] = w_ref[...].astype(BF)
-    bias_buf[spot([])] = bias_ref[...]
+    share = q_bias_ref.shape[1]
+    bias_own = jnp.concatenate(
+        [q_bias_ref[...], w_bias_ref[...], jnp.zeros((1, 128 - 2 * share), F32)], axis=1
+    )
+    bias_buf[spot([])] = jnp.broadcast_to(bias_own, (8, 128))
     greet(comm, sub, comms, subs)
     begin("q", 0)
     begin("bias", 0)
@@ -352,14 +363,20 @@
     def _(n):
         happen("build", n)
         build_rows(
-            index_ref, count_ref, importance_ref, own_mix, halo_ref, n * 128, rows=rows, halo=halo
+            index_ref,
+            count_ref[pl.ds(n, 1), :],
+            importance_ref,
+            own_mix,
+            halo_ref,
+            n * 128,
+            rows=rows,
+            halo=halo,
         )
         give(0, place(n, 128))
 
     finish("q", last)
     finish("bias", last)
     q_local.start()
-    share = width >> bits
     for k in range(2):
         pieces = []
         for e in range(1 << bits):
@@ -417,8 +434,7 @@
     block, pool_block = 256, 384
     q_rows, w_rows = q_weight.shape[0], w_weight.shape[0]
     share = q_bias.shape[0]
-    bias_tile = jnp.pad(jnp.concatenate([q_bias, w_bias])[None], ((0, 7), (0, 128 - 2 * share)))
-    by_sub = send_rows.reshape(comms, subs, per).transpose(1, 0, 2).reshape(halo, 1)
+    targets = send_targets(send_rows, comms, subs)
     lead = (2,) * bits
 
     here = pl.BlockSpec(memory_space=pltpu.VMEM)
@@ -428,7 +444,7 @@
         functools.partial(
             gather_kernel, comms=comms, subs=subs, bits=bits, block=block, pool_block=pool_block
         ),
-        in_specs=[here] * 7 + [anywhere],
+        in_specs=[here] * 8 + [anywhere],
         out_specs=[anywhere, here, anywhere, anywhere, anywhere, here, anywhere, anywhere, here],
         out_shape=[
             jax.ShapeDtypeStruct((rows, rows), BF),
@@ -471,12 +487,13 @@
         name="gather_and_transform",
     )(
         nbr_index.T,
-        nbr_count.reshape(1, rows),
+        nbr_count.reshape(rows // 128, 128),
         importance.T,
         q_weight,
         w_weight,
-        bias_tile,
-        by_sub,
+        q_bias.reshape(1, share),
+        w_bias.reshape(1, share),
+        targets,
         features,
     )
     own_mix, halo_mix, low, slope, pooled_own, incoming, q_full, w_full, biases = out
@@ -489,8 +506,7 @@
         incoming,
         q_full.reshape(devices * q_rows, width),
         w_full.reshape(devices * w_rows, width),
-        biases[0],
-        biases[1],
+        biases,
     )
 
 
@@ -510,7 +526,8 @@
     sent = neigh[send_rows[0]]
     incoming = lax.all_to_all(sent, AXES, split_axis=0, concat_axis=0, tiled=True).reshape(halo, width)
     pooled_own = pool_own(own_mix, neigh)
-    return own_mix, halo_mix, low, slope.astype(BF), pooled_own, incoming, q_full, w_full, qbias_full, wbias_full
+    biases = jnp.pad(jnp.stack([qbias_full, wbias_full]), ((0, 6), (0, 0)))
+    return own_mix, halo_mix, low, slope.astype(BF), pooled_own, incoming, q_full, w_full, biases
 
 
 def resident(*shape):
@@ -576,7 +593,7 @@
         at = slice(c, c + chunk)
         pre = jnp.dot(low_ref[...], w_ref[:width, at], preferred_element_type=F32)
         pre += jnp.dot(pooled_ref[...], w_ref[width:, at], preferred_element_type=F32)
-        act, slope = gelu_pair(pre + bias_ref[:, at])
+        act, slope = gelu_pair(pre + bias_ref[1:2, at])
         act_buf[:, at] = act
         slope_buf[:, at] = slope
         square = act * act
@@ -607,10 +624,10 @@
     )
 
 
-def combine(pooled_own, halo_mix, incoming, low, w_full, w_bias, cotangent):
+def combine(pooled_own, halo_mix, incoming, low, w_full, biases, cotangent):
     rows, width = low.shape
     halo = incoming.shape[0]
-    block = 256
+    block = 768
     return pl.pallas_call(
         combine_kernel,
         grid=(rows // block,),
@@ -620,7 +637,7 @@
             resident(halo, width),
             by_rows(block, width),
             resident(2 * width, width),
-            resident(1, width),
+            resident(8, width),
             by_rows(block, width),
         ],
         out_specs=[
@@ -645,7 +662,7 @@
             flops=6 * rows * width * width, bytes_accessed=22 * rows * width, transcendentals=rows * width
         ),
         name="combine",
-    )(pooled_own, halo_mix, incoming, low, w_full, w_bias.reshape(1, width), cotangent)
+    )(pooled_own, halo_mix, incoming, low, w_full, biases, cotangent)
 
 
 def swap(x, bit, devices):
@@ -750,13 +767,10 @@
     def top_index(self, top):
         return ((top // 2) % 2, top % 2)
 
-    def later(self, k):
-        out = []
-        for h in range(2):
-            n = 4 + 2 * (k - 1) + h
-            at = (h,) + (slice(self.offset(k), self.offset(k) + (1 << (self.bits - 1 - k))),)
-            out.append(self.copy(n, self.next_sent.at[at], self.next_got.at[at], self.orders[h][k - 1]))
-        return out
+    def later(self, k, h):
+        n = 4 + 2 * (k - 1) + h
+        at = (h, slice(self.offset(k), self.offset(k) + (1 << (self.bits - 1 - k))))
+        return self.copy(n, self.next_sent.at[at], self.next_got.at[at], self.orders[h][k - 1])
 
     def offset(self, k):
         return (1 << (self.bits - 1)) - (1 << (self.bits - k))
@@ -764,8 +778,8 @@
     def spot(self, chosen):
         return tuple(chosen[b] for b in self.lead)
 
-    def absorb(self, k):
-        for h in range(2):
+    def absorb(self, k, halves):
+        for h in halves:
             order = self.orders[h]
             fixed = order[:k]
             free = [b for b in self.lead if b not in fixed]
@@ -803,13 +817,16 @@
 
             lax.fori_loop(0, 1 << len(others), body, 0)
 
-    def start(self, k):
-        for c in self.later(k):
-            c.start()
-
-    def wait(self, k):
-        for c in [self.first(t) for t in range(4)] if k == 0 else self.later(k):
-            c.wait()
+    def advance(self, k):
+        if k == 0:
+            for t in range(4):
+                self.first(t).wait()
+        for h in range(2):
+            if k > 0:
+                self.later(k, h).wait()
+            self.absorb(k, [h])
+            if k < self.bits - 1:
+                self.later(k + 1, h).start()
 
     def result(self):
         return self.held[self.spot({b: self.mine[b] for b in self.lead})]
@@ -912,12 +929,6 @@
         at = pl.ds(pl.multiple_of(n * row_block, row_block), row_block)
         return pltpu.make_async_copy(features.at[n % 2], features_out.at[at, :], out_sem.at[n % 2])
 
-    def step_of(which, k):
-        which.wait(k)
-        which.absorb(k)
-        if k < bits - 1:
-            which.start(k + 1)
-
     def deal(value, which, top, rows_each):
         keep_even = mine[0] == 0
         shares = value.shape[0] // rows_each
@@ -939,8 +950,9 @@
         ("spread", 5): [(0, 3)],
         ("q", 1): [(1, 2), (0, 4)],
         ("q", 3): [(1, 3)],
-        ("features", 1): [(1, 4), (2, 0)],
-        ("features", 4): [(2, 1)],
+        ("features", 1): [(2, 0)],
+        ("features", 3): [(1, 4)],
+        ("features", 5): [(2, 1)],
     }
     all_sets = w_sets + [q_set]
 
@@ -951,7 +963,7 @@
                 @pl.when(n == step)
                 def _(which=which):
                     for m, k in which:
-                        step_of(all_sets[m], k)
+                        all_sets[m].advance(k)
 
     def load_when(step, n, begin=(), need=()):
         @pl.when(n == step)
@@ -1063,7 +1075,7 @@
             q_set.first(2 * j).start()
             q_set.first(2 * j + 1).start()
         for m, k in events.get(("q", t), []):
-            step_of(all_sets[m], k)
+            all_sets[m].advance(k)
     bias_step(4)
     for n in (8, 9):
         loads[n].wait()
@@ -1084,13 +1096,31 @@
         out_copy(n).start()
 
     for k in range(2, bits):
-        step_of(q_set, k)
+        q_set.advance(k)
     for n in range(2):
         w_out[:, n * half : (n + 1) * half] = w_sets[n].result()
     q_out[...] = q_set.result()
     bias_step(bits)
     for n in range(rounds - 2, rounds):
         out_copy(n).wait()
+
+
+def settle_kernel(source_ref, target_ref):
+    target_ref[...] = source_ref[...]
+
+
+def settle(x):
+    rows, width = x.shape
+    block = 384
+    return pl.pallas_call(
+        settle_kernel,
+        grid=(rows // block,),
+        in_specs=[by_rows(block, width)],
+        out_specs=by_rows(block, width),
+        out_shape=jax.ShapeDtypeStruct(x.shape, x.dtype),
+        compiler_params=pltpu.CompilerParams(vmem_limit_bytes=62 * 2**20),
+        name="settle",
+    )(x)
 
 
 def back_kernel(
@@ -1104,7 +1134,7 @@
     halo = devices * per
     mix_block, row_block = 384, 384
     w_rows, q_rows = w_full.shape[0] // devices, q_full.shape[0] // devices
-    targets = send_rows.reshape(comms, subs, per).transpose(1, 0, 2).reshape(1, halo)
+    targets = send_targets(send_rows, comms, subs)
     lead = (2,) * (bits - 1)
 
     def set_scratch(rows_each, columns):
@@ -1172,7 +1202,7 @@
     )(sent_grad, grad_wbias, targets, own_mix, slope, low, pooled, grad_out, grad_pooled, w_full, q_full)
     share = width // devices
     sums = lax.dynamic_slice_in_dim(biases.reshape(2, width), lax.axis_index(AXES) * share, share, 1)
-    return grad_features, grad_q, sums[1], grad_w, sums[0]
+    return settle(grad_features), grad_q, sums[1], grad_w, sums[0]
 
 
 def shards(
@@ -1190,11 +1220,11 @@
     devices = lax.axis_size(AXES)
     kernel_fits = devices == 32 and q_weight.shape[0] % 16 == 0
     gather, back = (gather_and_transform, back_kernel) if kernel_fits else (gather_plain, back_plain)
-    own_mix, halo_mix, low, slope, pooled_own, incoming, q_full, w_full, qbias_full, wbias_full = gather(
+    own_mix, halo_mix, low, slope, pooled_own, incoming, q_full, w_full, biases = gather(
         features, q_weight, q_bias, w_weight, w_bias, nbr_index, nbr_count, importance, send_rows
     )
     embedding, pooled, grad_out, grad_pooled, sent_grad, grad_wbias = combine(
-        pooled_own, halo_mix, incoming, low, w_full, wbias_full, cotangent
+        pooled_own, halo_mix, incoming, low, w_full, biases, cotangent
     )
     grad_features, grad_q, grad_qbias, grad_w, grad_wbias = back(
         own_mix, low, slope, pooled, grad_out, grad_pooled, sent_grad, grad_wbias, q_full, w_full, send_rows

time: 183 us -> 175 us (0.956)
  local copies, waits for them, and re-layouts: 17.6 us -> 3.5 us
  Pallas kernels: 164 us -> 171 us
    unnamed x7 -> x8, local copies, waits for them, and re-layouts: 10.8 us -> 1.37 us
    pallas_call x0 -> x1, Pallas kernels: none -> 8.69 us  [settle(): pl.pallas_call(settle_kernel, grid=(rows // block,), in_specs=[by_rows(bl...]
    pallas_call x1, Pallas kernels: 31.2 us -> 28.7 us  [combine(): pl.pallas_call(combine_kernel, grid=(rows // block,), in_specs=[by_rows(b...]
    reshape x4 -> x2, local copies, waits for them, and re-layouts: 3.4 us -> 1.38 us  [send_targets(): send_rows.reshape(comms, subs, per).transpose(1, 0, 2)]
where the time goes in v3:
time: 175 us
  Pallas kernels  171 us (98%)
  local copies, waits for them, and re-layouts  3.5 us (2%)
    pallas_call x1, Pallas kernels, back_kernel(): pl.pallas_call(functools.partial(back_body, comms=comms, subs=subs, bits=...  70.6 us
    pallas_call x1, Pallas kernels, gather_and_transform(): pl.pallas_call(functools.partial(gather_kernel, comms=comms, subs=subs, b...  62.7 us
    pallas_call x1, Pallas kernels, combine(): pl.pallas_call(combine_kernel, grid=(rows // block,), in_specs=[by_rows(b...  28.7 us
    pallas_call x1, Pallas kernels, settle(): pl.pallas_call(settle_kernel, grid=(rows // block,), in_specs=[by_rows(bl...  8.69 us

profile of v3, /device:TPU:0, one launch (start us, length us, event | category | flops | bytes accessed | tf_op | source)
XLA Modules:
  0.0 174.9 jit_solution(16195772629690268866)
XLA Ops:
  0.6 0.8 reshape.41
  1.4 0.1 copy.17
  1.5 0.6 reshape.42.send_ref.target_ref
  2.2 62.7 %gather_and_transform.1 = (bf16[2304,2304]{1,0:T(8,128)(2,1)}, bf16[2304,128]{1,0:T(8,128)(2,1)}, bf16[2304,1024]{1,0:T(8,128)(2,1)}, bf16[2304,1024]{1,0:T(8,12...) custom-call(s32[50,2304]{1,0:T(8,128)} %bitcast.17, ...), custom_call_target="tpu_custom_call" | custom-call | tf_op jit(solution)/shard_map/gather_and_transform/pallas_call | solution.py:443
  64.9 28.7 %combine.1 = (f32[2304,1024]{1,0:T(8,128)}, bf16[2304,1024]{1,0:T(8,128)(2,1)}, bf16[2304,1024]{1,0:T(8,128)(2,1)}, bf16[2304,1024]{1,0:T(8,128)(2,1)}, f32[128,1024]{1,0:T(8,128)}, /*index=5*/f32[8,1024]{1,0:T(8,128)}) custom-call(f32[2304,1024]{1,0:T(8,128)} %get-tuple-element.25.own_ref, bf16[2304,128]{1,0:T(8,128)(2,1)} %get-tuple-element.26.halo_ref, ...), custom_call_target="tpu_custom_call" | custom-call | flops 14495514624 | bytes 51904512 | tf_op jit(solution)/shard_map/combine/pallas_call | solution.py:631
  93.5 70.6 %back.1 = (f32[2304,1024]{1,0:T(8,128)}, f32[32,1024]{1,0:T(8,128)}, f32[64,1024]{1,0:T(8,128)}, f32[16,128]{1,0:T(8,128)}) custom-call(f32[128,1024]{1,0:T(8,128)} %get-tuple-element.32.sent_grad_ref, f32[8,1024]{1,0:T(8,128)} %get-tuple-element.33.w_bias_ref, s32[1,128]{1,0:T(1,128)} %reshape.42.send_ref.target_ref, ...), custom_call_target="tpu_custom_call" | custom-call | tf_op jit(solution)/shard_map/back/pallas_call | solution.py:1155
  164.2 0.0 copy-start.2
  164.2 0.0 copy-start.1
  164.2 0.0 copy-start
  164.2 8.7 %settle.1 = f32[2304,1024]{1,0:T(8,128)} custom-call(f32[2304,1024]{1,0:T(8,128)} %get-tuple-element.40.source_ref), custom_call_target="tpu_custom_call" | custom-call | tf_op jit(solution)/shard_map/settle/pallas_call | solution.py:1115
  172.9 0.0 copy-done.2
  172.9 0.1 constant_dynamic-slice_fusion
  173.0 0.5 slice_bitcast_fusion
  173.5 0.0 copy-done.1
  173.5 0.7 copy.20
  174.2 0.0 copy-done
  174.2 0.7 copy.21
  (1 shorter events, 0.0 us)
Async XLA Ops:
  164.2 8.7 %copy-start.2 = (f32[16,128]{1,0:T(8,128)S(1)}, f32[16,128]{1,0:T(8,128)}, u32[]{:S(2)}) copy-start(f32[16,128]{1,0:T(8,128)} %get-tuple-element.42) | copy-start | bytes 24580
  164.2 9.3 %copy-start.1 = (f32[32,1024]{1,0:T(8,128)S(1)}, f32[32,1024]{1,0:T(8,128)}, u32[]{:S(2)}) copy-start(f32[32,1024]{1,0:T(8,128)} %get-tuple-element.54) | copy-start | bytes 393220
  164.2 10.0 %copy-start = (f32[64,1024]{1,0:T(8,128)S(1)}, f32[64,1024]{1,0:T(8,128)}, u32[]{:S(2)}) copy-start(f32[64,1024]{1,0:T(8,128)} %get-tuple-element.56) | copy-start | bytes 786436

commit v4 on v3

--- a/solution.py
+++ b/solution.py
@@ -112,10 +112,9 @@
 def gelu_pair(x):
     c = math.sqrt(2.0 / math.pi)
     square = x * x
-    t = jnp.tanh(x * (c + (c * 0.044715) * square))
-    half = 0.5 + 0.5 * t
-    slope = x * (0.5 - 0.5 * t * t) * (c + (3.0 * c * 0.044715) * square)
-    return x * half, half + slope
+    half = 0.5 + 0.5 * jnp.tanh(x * (c + (c * 0.044715) * square))
+    value = x * half
+    return value, half + value * (1.0 - half) * (2.0 * c + (6.0 * c * 0.044715) * square)
 
 
 def hidden_rows(features_ref, q_buf, bias_ref, send_ref, low_ref, neigh_ref, slope_ref, sent_ref, at_rows, start):
@@ -194,7 +193,6 @@
     low_out,
     slope_out,
     pooled_out,
-    incoming_ref,
     q_full,
     w_full,
     bias_out,
@@ -204,6 +202,7 @@
     neigh,
     slope,
     pooled,
+    pooled_low,
     q_buf,
     w_own,
     bias_buf,
@@ -306,7 +305,7 @@
         at = place(n, block)
         return pltpu.make_async_copy(features_hbm.at[at, :], features.at[at, :], feature_sem.at[n])
 
-    outs = [(own_mix, own_out), (low, low_out), (slope, slope_out), (pooled, pooled_out)]
+    outs = [(own_mix, own_out), (low, low_out), (slope, slope_out), (pooled_low, pooled_out)]
 
     def give(n, at):
         source, target = outs[n]
@@ -412,12 +411,19 @@
 
         at = place(n, pool_block)
         pooled[at, :] = jnp.dot(own_mix[at, :], neigh[...], preferred_element_type=F32)
+
+    finish("comm", 0)
+
+    @pl.loop(0, rows // pool_block)
+    def _(n):
+        at = place(n, pool_block)
+        received = comm_landed[...].reshape(halo, width)
+        total = pooled[at, :] + jnp.dot(halo_ref[at, :], received, preferred_element_type=F32)
+        pooled_low[at, :] = total.astype(BF)
         give(3, at)
 
     finish("w0", last)
     finish("w1", last)
-    finish("comm", 0)
-    incoming_ref[...] = comm_landed[...].reshape(halo, width)
     q_local.wait()
     for n in range(4):
         given(n)
@@ -445,14 +451,13 @@
             gather_kernel, comms=comms, subs=subs, bits=bits, block=block, pool_block=pool_block
         ),
         in_specs=[here] * 8 + [anywhere],
-        out_specs=[anywhere, here, anywhere, anywhere, anywhere, here, anywhere, anywhere, here],
+        out_specs=[anywhere, here, anywhere, anywhere, anywhere, anywhere, anywhere, here],
         out_shape=[
             jax.ShapeDtypeStruct((rows, rows), BF),
             jax.ShapeDtypeStruct((rows, halo), BF),
             jax.ShapeDtypeStruct((rows, width), BF),
             jax.ShapeDtypeStruct((rows, width), BF),
-            jax.ShapeDtypeStruct((rows, width), F32),
-            jax.ShapeDtypeStruct((halo, width), BF),
+            jax.ShapeDtypeStruct((rows, width), BF),
             jax.ShapeDtypeStruct(lead + (q_rows, width), BF),
             jax.ShapeDtypeStruct(lead + (w_rows, width), BF),
             jax.ShapeDtypeStruct((8, width), F32),
@@ -464,6 +469,7 @@
             pltpu.VMEM((rows, width), BF),
             pltpu.VMEM((rows, width), BF),
             pltpu.VMEM((rows, width), F32),
+            pltpu.VMEM((rows, width), BF),
             pltpu.VMEM(lead + (q_rows, width), BF),
             pltpu.VMEM((w_rows, width), BF),
             pltpu.VMEM(lead + (8, 128), F32),
@@ -496,14 +502,13 @@
         targets,
         features,
     )
-    own_mix, halo_mix, low, slope, pooled_own, incoming, q_full, w_full, biases = out
+    own_mix, halo_mix, low, slope, pooled, q_full, w_full, biases = out
     return (
         own_mix,
         halo_mix,
         low,
         slope,
-        pooled_own,
-        incoming,
+        pooled,
         q_full.reshape(devices * q_rows, width),
         w_full.reshape(devices * w_rows, width),
         biases,
@@ -525,9 +530,9 @@
     neigh = neigh.astype(BF)
     sent = neigh[send_rows[0]]
     incoming = lax.all_to_all(sent, AXES, split_axis=0, concat_axis=0, tiled=True).reshape(halo, width)
-    pooled_own = pool_own(own_mix, neigh)
+    pooled = pool_own(own_mix, neigh) + jnp.dot(halo_mix, incoming, preferred_element_type=F32)
     biases = jnp.pad(jnp.stack([qbias_full, wbias_full]), ((0, 6), (0, 0)))
-    return own_mix, halo_mix, low, slope.astype(BF), pooled_own, incoming, q_full, w_full, biases
+    return own_mix, halo_mix, low, slope.astype(BF), pooled.astype(BF), q_full, w_full, biases
 
 
 def resident(*shape):
@@ -560,15 +565,13 @@
 
 
 def combine_kernel(
-    own_ref,
+    pooled_ref,
     halo_ref,
-    incoming_ref,
     low_ref,
     w_ref,
     bias_ref,
     cotangent_ref,
     embedding_ref,
-    pooled_ref,
     grad_ref,
     grad_pooled_ref,
     sent_ref,
@@ -585,8 +588,6 @@
         sent_ref[...] = jnp.zeros_like(sent_ref)
         bias_grad_ref[...] = jnp.zeros_like(bias_grad_ref)
 
-    pooled = own_ref[...] + jnp.dot(halo_ref[...], incoming_ref[...], preferred_element_type=F32)
-    pooled_ref[...] = pooled.astype(BF)
     squares = jnp.zeros((block, 128), F32)
     dots = jnp.zeros((block, 128), F32)
     for c in range(0, width, chunk):
@@ -624,9 +625,9 @@
     )
 
 
-def combine(pooled_own, halo_mix, incoming, low, w_full, biases, cotangent):
+def combine(pooled, halo_mix, low, w_full, biases, cotangent):
     rows, width = low.shape
-    halo = incoming.shape[0]
+    halo = halo_mix.shape[1]
     block = 768
     return pl.pallas_call(
         combine_kernel,
@@ -634,7 +635,6 @@
         in_specs=[
             by_rows(block, width),
             by_rows(block, halo),
-            resident(halo, width),
             by_rows(block, width),
             resident(2 * width, width),
             resident(8, width),
@@ -644,13 +644,11 @@
             by_rows(block, width),
             by_rows(block, width),
             by_rows(block, width),
-            by_rows(block, width),
             pl.BlockSpec((halo, width), lambda i: (0, 0)),
             pl.BlockSpec((8, width), lambda i: (0, 0)),
         ],
         out_shape=[
             jax.ShapeDtypeStruct((rows, width), F32),
-            jax.ShapeDtypeStruct((rows, width), BF),
             jax.ShapeDtypeStruct((rows, width), BF),
             jax.ShapeDtypeStruct((rows, width), BF),
             jax.ShapeDtypeStruct((halo, width), F32),
@@ -662,7 +660,7 @@
             flops=6 * rows * width * width, bytes_accessed=22 * rows * width, transcendentals=rows * width
         ),
         name="combine",
-    )(pooled_own, halo_mix, incoming, low, w_full, biases, cotangent)
+    )(pooled, halo_mix, low, w_full, biases, cotangent)
 
 
 def swap(x, bit, devices):
@@ -870,8 +868,8 @@
     mix_block,
     row_block,
 ):
-    sets = [rest[7 * k : 7 * k + 7] for k in range(3)]
-    load_sem, mix_sem, out_sem, bias_send, bias_recv, comm_send, comm_recv, sub_send, sub_recv = rest[21:]
+    sets = [rest[7 * k : 7 * k + 7] for k in range(4)]
+    load_sem, mix_sem, out_sem, bias_send, bias_recv, comm_send, comm_recv, sub_send, sub_recv = rest[28:]
     rows, width = grad_out.shape
     halo = sent_grad_ref.shape[0]
     half = width // 2
@@ -888,7 +886,7 @@
     high = list(range(3, bits))
     orders = ([1, 2] + high, [2, 1] + high)
     w_sets = [ScatterSum(sets[k], orders, mine, partner) for k in range(2)]
-    q_set = ScatterSum(sets[2], orders, mine, partner)
+    q_sets = [ScatterSum(sets[2 + k], orders, mine, partner) for k in range(2)]
 
     left, right = pl.ds(0, half), pl.ds(half, half)
     loads = [
@@ -944,17 +942,17 @@
 
     events = {
         ("w1", 1): [(0, 0)],
-        ("spread", 1): [(1, 0), (0, 1)],
+        ("spread", 1): [(0, 1), (1, 0)],
         ("spread", 3): [(0, 2)],
-        ("spread", 4): [(1, 1)],
-        ("spread", 5): [(0, 3)],
-        ("q", 1): [(1, 2), (0, 4)],
-        ("q", 3): [(1, 3)],
-        ("features", 1): [(2, 0)],
-        ("features", 3): [(1, 4)],
-        ("features", 5): [(2, 1)],
+        ("spread", 5): [(1, 1), (0, 3)],
+        ("q", 1): [(0, 4)],
+        ("q", 2): [(2, 0), (1, 2)],
+        ("features", 0): [(3, 0)],
+        ("features", 2): [(1, 3), (2, 1)],
+        ("features", 4): [(3, 1), (2, 2)],
+        ("features", 5): [(1, 4)],
     }
-    all_sets = w_sets + [q_set]
+    all_sets = w_sets + q_sets
 
     def happen(phase, n):
         for (when, step), which in events.items():
@@ -1055,25 +1053,16 @@
 
     for t in range(4):
         bias_step(t)
-        n, j = t % 2, t // 2
+        n, j = t // 2, t % 2
         value = lax.dot_general(
             joined[:, j * half : (j + 1) * half],
             joined[:, width + n * half : width + (n + 1) * half],
             tn,
             preferred_element_type=F32,
         )
-        keep_even = mine[0] == 0
-        columns = slice(n * half, (n + 1) * half)
-        each = q_out.shape[0]
-        for p in range(half // each // 2):
-            even = value[2 * p * each : (2 * p + 1) * each]
-            odd = value[(2 * p + 1) * each : (2 * p + 2) * each]
-            at = (j, (p >> 2) & 1, (p >> 1) & 1, p & 1, slice(None), columns)
-            q_set.held[at] = jnp.where(keep_even, even, odd)
-            q_set.sent[at] = jnp.where(keep_even, odd, even).astype(BF)
-        if n == 1:
-            q_set.first(2 * j).start()
-            q_set.first(2 * j + 1).start()
+        deal(value, q_sets[n], (j,), q_out.shape[0])
+        q_sets[n].first(2 * j).start()
+        q_sets[n].first(2 * j + 1).start()
         for m, k in events.get(("q", t), []):
             all_sets[m].advance(k)
     bias_step(4)
@@ -1095,11 +1084,11 @@
         )
         out_copy(n).start()
 
-    for k in range(2, bits):
-        q_set.advance(k)
+    for n, k in ((1, 2), (0, 3), (1, 3), (0, 4), (1, 4)):
+        q_sets[n].advance(k)
     for n in range(2):
         w_out[:, n * half : (n + 1) * half] = w_sets[n].result()
-    q_out[...] = q_set.result()
+        q_out[:, n * half : (n + 1) * half] = q_sets[n].result()
     bias_step(bits)
     for n in range(rounds - 2, rounds):
         out_copy(n).wait()
@@ -1111,7 +1100,7 @@
 
 def settle(x):
     rows, width = x.shape
-    block = 384
+    block = rows // 2
     return pl.pallas_call(
         settle_kernel,
         grid=(rows // block,),
@@ -1183,7 +1172,8 @@
         ]
         + set_scratch(w_rows, width // 2)
         + set_scratch(w_rows, width // 2)
-        + set_scratch(q_rows, width)
+        + set_scratch(q_rows, width // 2)
+        + set_scratch(q_rows, width // 2)
         + [
             pltpu.SemaphoreType.DMA((10,)),
             pltpu.SemaphoreType.DMA((2,)),
@@ -1220,11 +1210,11 @@
     devices = lax.axis_size(AXES)
     kernel_fits = devices == 32 and q_weight.shape[0] % 16 == 0
     gather, back = (gather_and_transform, back_kernel) if kernel_fits else (gather_plain, back_plain)
-    own_mix, halo_mix, low, slope, pooled_own, incoming, q_full, w_full, biases = gather(
+    own_mix, halo_mix, low, slope, pooled, q_full, w_full, biases = gather(
         features, q_weight, q_bias, w_weight, w_bias, nbr_index, nbr_count, importance, send_rows
     )
-    embedding, pooled, grad_out, grad_pooled, sent_grad, grad_wbias = combine(
-        pooled_own, halo_mix, incoming, low, w_full, biases, cotangent
+    embedding, grad_out, grad_pooled, sent_grad, grad_wbias = combine(
+        pooled, halo_mix, low, w_full, biases, cotangent
     )
     grad_features, grad_q, grad_qbias, grad_w, grad_wbias = back(
         own_mix, low, slope, pooled, grad_out, grad_pooled, sent_grad, grad_wbias, q_full, w_full, send_rows

time: 175 us -> 167 us (0.954)
  Pallas kernels: 171 us -> 163 us
    pallas_call x1, Pallas kernels: 70.6 us -> 64.6 us  [back_kernel(): pl.pallas_call(functools.partial(back_body, comms=comms, subs=subs, bits=...]
    pallas_call x1, Pallas kernels: 8.69 us -> 6.58 us  [settle(): pl.pallas_call(settle_kernel, grid=(rows // block,), in_specs=[by_rows(bl...]
where the time goes in v4:
time: 167 us
  Pallas kernels  163 us (98%)
  local copies, waits for them, and re-layouts  3.5 us (2%)
    pallas_call x1, Pallas kernels, back_kernel(): pl.pallas_call(functools.partial(back_body, comms=comms, subs=subs, bits=...  64.6 us
    pallas_call x1, Pallas kernels, gather_and_transform(): pl.pallas_call(functools.partial(gather_kernel, comms=comms, subs=subs, b...  64.3 us
    pallas_call x1, Pallas kernels, combine(): pl.pallas_call(combine_kernel, grid=(rows // block,), in_specs=[by_rows(b...  27.2 us
    pallas_call x1, Pallas kernels, settle(): pl.pallas_call(settle_kernel, grid=(rows // block,), in_specs=[by_rows(bl...  6.58 us

profile of v4, /device:TPU:0, one launch (start us, length us, event | category | flops | bytes accessed | tf_op | source)
XLA Modules:
  0.0 166.8 jit_solution(4385946609522772970)
XLA Ops:
  0.6 0.8 reshape.41
  1.4 0.1 copy.17
  1.5 0.6 reshape.42.send_ref.target_ref
  2.2 64.3 %gather_and_transform.1 = (bf16[2304,2304]{1,0:T(8,128)(2,1)}, bf16[2304,128]{1,0:T(8,128)(2,1)}, bf16[2304,1024]{1,0:T(8,128)(2,1)}, bf16[2304,1024]{1,0:T(8,12...) custom-call(s32[50,2304]{1,0:T(8,128)} %bitcast.17, ...), custom_call_target="tpu_custom_call" | custom-call | tf_op jit(solution)/shard_map/gather_and_transform/pallas_call | solution.py:449
  66.5 27.2 %combine.1 = (f32[2304,1024]{1,0:T(8,128)}, bf16[2304,1024]{1,0:T(8,128)(2,1)}, bf16[2304,1024]{1,0:T(8,128)(2,1)}, f32[128,1024]{1,0:T(8,128)}, f32[8,1024]{1,0:T(8,128)}) custom-call(bf16[2304,1024]{1,0:T(8,128)(2,1)} %get-tuple-element.23.pooled_ref.pooled_hbm, bf16[2304,128]{1,0:T(8,128)(2,1)} %get-tuple-element.24.halo_ref, ...), custom_call_target="tpu_custom_call" | custom-call | flops 14495514624 | bytes 51904512 | tf_op jit(solution)/shard_map/combine/pallas_call | solution.py:632
  93.6 64.6 %back.1 = (f32[2304,1024]{1,0:T(8,128)}, f32[32,1024]{1,0:T(8,128)}, f32[64,1024]{1,0:T(8,128)}, f32[16,128]{1,0:T(8,128)}) custom-call(f32[128,1024]{1,0:T(8,128)} %get-tuple-element.29.sent_grad_ref, f32[8,1024]{1,0:T(8,128)} %get-tuple-element.30.w_bias_ref, s32[1,128]{1,0:T(1,128)} %reshape.42.send_ref.target_ref, ...), custom_call_target="tpu_custom_call" | custom-call | tf_op jit(solution)/shard_map/back/pallas_call | solution.py:1144
  158.2 0.0 copy-start.2
  158.2 0.0 copy-start.1
  158.2 0.0 copy-start
  158.2 6.6 %settle.1 = f32[2304,1024]{1,0:T(8,128)} custom-call(f32[2304,1024]{1,0:T(8,128)} %get-tuple-element.36.source_ref), custom_call_target="tpu_custom_call" | custom-call | tf_op jit(solution)/shard_map/settle/pallas_call | solution.py:1104
  164.8 0.0 copy-done.2
  164.8 0.1 constant_dynamic-slice_fusion
  164.9 0.5 slice_bitcast_fusion
  165.4 0.0 copy-done.1
  165.4 0.7 copy.20
  166.1 0.0 copy-done
  166.1 0.7 copy.21
  (1 shorter events, 0.0 us)
Async XLA Ops:
  158.2 6.6 %copy-start.2 = (f32[16,128]{1,0:T(8,128)S(1)}, f32[16,128]{1,0:T(8,128)}, u32[]{:S(2)}) copy-start(f32[16,128]{1,0:T(8,128)} %get-tuple-element.38) | copy-start | bytes 24580
  158.2 7.2 %copy-start.1 = (f32[32,1024]{1,0:T(8,128)S(1)}, f32[32,1024]{1,0:T(8,128)}, u32[]{:S(2)}) copy-start(f32[32,1024]{1,0:T(8,128)} %get-tuple-element.50) | copy-start | bytes 393220
  158.2 7.9 %copy-start = (f32[64,1024]{1,0:T(8,128)S(1)}, f32[64,1024]{1,0:T(8,128)}, u32[]{:S(2)}) copy-start(f32[64,1024]{1,0:T(8,128)} %get-tuple-element.52) | copy-start | bytes 786436

commit v5 on v4

--- a/solution.py
+++ b/solution.py
@@ -276,13 +276,28 @@
         groups.append([exchange(buf, 0, done + [1, 2], part)])
         return groups
 
+    def chain_xy(buf, own, part):
+        groups = [
+            [
+                exchange(buf, 1, [], part, left, own.at[part, left]),
+                exchange(buf, 2, [], part, right, own.at[part, right]),
+            ],
+            [exchange(buf, 2, [1], part, left), exchange(buf, 1, [2], part, right)],
+        ]
+        done = [1, 2]
+        for b in high:
+            groups.append([exchange(buf, b, done, part)])
+            done = done + [b]
+        groups.append([exchange(buf, 0, done, part)])
+        return groups
+
     w_rows = w_own.shape[0]
     top, bottom = pl.ds(0, w_rows // 2), pl.ds(w_rows // 2, w_rows // 2)
     chains = {
         "q": chain(q_buf, None, True),
         "bias": chain(bias_buf, None, False),
         "w0": chain(w_full, w_own.at[top], True, top),
-        "w1": chain(w_full, w_own.at[bottom], True, bottom),
+        "w1": chain_xy(w_full, w_own, bottom),
         "sub": [ring_copies(subs, sub, sub_blocks, sub_landed, sub_send, sub_recv, lambda j: (comm, j))],
         "comm": [ring_copies(comms, comm, comm_blocks, comm_landed, comm_send, comm_recv, lambda j: (j, sub))],
     }
@@ -315,18 +330,17 @@
         pltpu.make_async_copy(*outs[n], local_sem.at[2 + n]).wait()
 
     events = {
-        ("build", 4): [("q", 0), ("bias", 0)],
+        ("build", 1): [("w1", -1)],
+        ("build", 4): [("q", 0), ("bias", 0), ("w1", 0)],
         ("build", 6): [("w0", -1)],
         ("build", 7): [("q", 1), ("bias", 1)],
-        ("build", 9): [("w1", -1)],
+        ("build", 9): [("w1", 1)],
         ("build", 10): [("q", 2), ("bias", 2), ("w0", 0)],
-        ("build", 13): [("w1", 0)],
-        ("build", 14): [("w0", 1)],
         ("build", 15): [("q", 3), ("bias", 3)],
-        ("hidden", 0): [("w1", 1)],
-        ("hidden", 1): [("w0", 2)],
-        ("hidden", 6): [("w0", 3), ("w1", 2)],
-        ("pool", 2): [("w1", 3)],
+        ("build", 16): [("w0", 1)],
+        ("hidden", 1): [("w1", 2), ("w0", 2)],
+        ("hidden", 6): [("w0", 3)],
+        ("pool", 1): [("w1", 3)],
     }
 
     def happen(phase, n):
@@ -1094,22 +1108,42 @@
         out_copy(n).wait()
 
 
-def settle_kernel(source_ref, target_ref):
-    target_ref[...] = source_ref[...]
-
-
-def settle(x):
-    rows, width = x.shape
+def settle_kernel(features_ref, q_ref, w_ref, biases_ref, features_out, q_out, w_out, q_bias_out, w_bias_out, *, subs):
+    features_out[...] = features_ref[...]
+
+    @pl.when(pl.program_id(0) == 0)
+    def _():
+        q_out[...] = q_ref[...]
+        w_out[...] = w_ref[...]
+        share = q_bias_out.shape[1]
+        each = 128 // share
+        me = lax.axis_index("comm") * subs + lax.axis_index("sub")
+        for first, target in ((0, w_bias_out), (8, q_bias_out)):
+            row = biases_ref[pl.ds(first + me // each, 1), :]
+            piece = row[:, :share]
+            for k in range(1, each):
+                piece = jnp.where(me % each == k, row[:, k * share : (k + 1) * share], piece)
+            target[...] = piece
+
+
+def settle(grad_features, grad_q, grad_w, biases):
+    rows, width = grad_features.shape
     block = rows // 2
+    share = grad_q.shape[0]
+    shapes = [grad_q.shape, grad_w.shape, (1, share), (1, share)]
+
+    def whole(shape):
+        return pl.BlockSpec(shape, lambda i: (0, 0))
+
     return pl.pallas_call(
-        settle_kernel,
+        functools.partial(settle_kernel, subs=lax.axis_size("sub")),
         grid=(rows // block,),
-        in_specs=[by_rows(block, width)],
-        out_specs=by_rows(block, width),
-        out_shape=jax.ShapeDtypeStruct(x.shape, x.dtype),
+        in_specs=[by_rows(block, width)] + [whole(x.shape) for x in (grad_q, grad_w, biases)],
+        out_specs=[by_rows(block, width)] + [whole(shape) for shape in shapes],
+        out_shape=[jax.ShapeDtypeStruct(shape, F32) for shape in [grad_features.shape] + shapes],
         compiler_params=pltpu.CompilerParams(vmem_limit_bytes=62 * 2**20),
         name="settle",
-    )(x)
+    )(grad_features, grad_q, grad_w, biases)
 
 
 def back_kernel(
@@ -1190,9 +1224,9 @@
         ),
         name="back",
     )(sent_grad, grad_wbias, targets, own_mix, slope, low, pooled, grad_out, grad_pooled, w_full, q_full)
+    grad_features, grad_q, grad_w, q_bias, w_bias = settle(grad_features, grad_q, grad_w, biases)
     share = width // devices
-    sums = lax.dynamic_slice_in_dim(biases.reshape(2, width), lax.axis_index(AXES) * share, share, 1)
-    return settle(grad_features), grad_q, sums[1], grad_w, sums[0]
+    return grad_features, grad_q, q_bias.reshape(share), grad_w, w_bias.reshape(share)
 
 
 def shards(

time: 167 us -> 164 us (0.982)
  local copies, waits for them, and re-layouts: 3.5 us -> 1.52 us
where the time goes in v5:
time: 164 us
  Pallas kernels  162 us (99%)
    pallas_call x1, Pallas kernels, back_kernel(): pl.pallas_call(functools.partial(back_body, comms=comms, subs=subs, bits=...  64.2 us
    pallas_call x1, Pallas kernels, gather_and_transform(): pl.pallas_call(functools.partial(gather_kernel, comms=comms, subs=subs, b...  63.6 us
    pallas_call x1, Pallas kernels, combine(): pl.pallas_call(combine_kernel, grid=(rows // block,), in_specs=[by_rows(b...  27.1 us
    pallas_call x1, Pallas kernels, settle(): pl.pallas_call(functools.partial(settle_kernel, subs=lax.axis_size('sub')...  6.84 us

profile of v5, /device:TPU:0, one launch (start us, length us, event | category | flops | bytes accessed | tf_op | source)
XLA Modules:
  0.0 164.0 jit_solution(16662802835441874595)
XLA Ops:
  0.6 0.8 reshape.44
  1.4 0.1 copy.17
  1.5 0.6 reshape.45.send_ref.target_ref
  2.2 63.6 %gather_and_transform.1 = (bf16[2304,2304]{1,0:T(8,128)(2,1)}, bf16[2304,128]{1,0:T(8,128)(2,1)}, bf16[2304,1024]{1,0:T(8,128)(2,1)}, bf16[2304,1024]{1,0:T(8,12...) custom-call(s32[50,2304]{1,0:T(8,128)} %bitcast.15, ...), custom_call_target="tpu_custom_call" | custom-call | tf_op jit(solution)/shard_map/gather_and_transform/pallas_call | solution.py:463
  65.8 27.1 %combine.1 = (f32[2304,1024]{1,0:T(8,128)}, bf16[2304,1024]{1,0:T(8,128)(2,1)}, bf16[2304,1024]{1,0:T(8,128)(2,1)}, f32[128,1024]{1,0:T(8,128)}, f32[8,1024]{1,0:T(8,128)}) custom-call(bf16[2304,1024]{1,0:T(8,128)(2,1)} %get-tuple-element.28.pooled_ref.pooled_hbm, bf16[2304,128]{1,0:T(8,128)(2,1)} %get-tuple-element.29.halo_ref, ...), custom_call_target="tpu_custom_call" | custom-call | flops 14495514624 | bytes 51904512 | tf_op jit(solution)/shard_map/combine/pallas_call | solution.py:646
  92.9 64.2 %back.1 = (f32[2304,1024]{1,0:T(8,128)}, f32[32,1024]{1,0:T(8,128)}, f32[64,1024]{1,0:T(8,128)}, f32[16,128]{1,0:T(8,128)}) custom-call(f32[128,1024]{1,0:T(8,128)} %get-tuple-element.34.sent_grad_ref, f32[8,1024]{1,0:T(8,128)} %get-tuple-element.35.w_bias_ref, s32[1,128]{1,0:T(1,128)} %reshape.45.send_ref.target_ref, ...), custom_call_target="tpu_custom_call" | custom-call | tf_op jit(solution)/shard_map/back/pallas_call | solution.py:1178
  157.1 6.8 %settle.1 = (f32[2304,1024]{1,0:T(8,128)}, f32[32,1024]{1,0:T(8,128)}, f32[64,1024]{1,0:T(8,128)}, f32[1,32]{1,0:T(1,128)}, f32[1,32]{1,0:T(1,128)}) custom-call(f32[2304,1024]{1,0:T(8,128)} %get-tuple-element.41.features_ref, f32[32,1024]{1,0:T(8,128)} %get-tuple-element.42.q_ref, f32[64,1024]{1,0:T(8,128)} %get-tuple-element.43.w_ref, ...), custom_call_target="tpu_custom_call" | custom-call | tf_op jit(solution)/shard_map/settle/pallas_call | solution.py:1138
